TPU v7x, 32 devices: a whole 2x2x4 slice. The times are simulated.
32 devices in a mesh: dp: 2 (over core), dom: 16 (over z, y, x).
Axes of the slice: x: 2, y: 2, z: 4, core: 2. Of those that a mesh axis runs over, the one named last changes fastest.
Arguments:
- density: bfloat16 [2, 64, 128, 256], P('dp', None, 'dom'), may hold values from -6 to 6
- upstream: bfloat16 [2, 64, 128, 256], P('dp', None, 'dom'), may hold values from -6 to 6
- spectral_weight: float32 [2048, 64], P(('dp', 'dom')), may hold values from -0.5 to 0.5
- moment_one: float32 [2048, 64], P(('dp', 'dom')), may hold values from -64 to 64
- moment_two: float32 [2048, 64], P(('dp', 'dom')), may hold values from 64 to 1024
- skip_weight: bfloat16 [64, 64], replicated, may hold values from -0.75 to 0.75
- skip_bias: float32 [64], replicated, may hold values from -3 to 3
- mode_counts: int32 [2], replicated, may hold values from 8 to 16, as said below
Outputs:
- input_grad: bfloat16 [2, 64, 128, 256], P('dp', None, 'dom')
- new_weight: float32 [2048, 64], P(('dp', 'dom'))
- new_moment_one: float32 [2048, 64], P(('dp', 'dom'))
- new_moment_two: float32 [2048, 64], P(('dp', 'dom'))
Inputs may be any that keep to these rules, and one draw needn't show every extreme that they name: `mode_counts`: some entry equals 16.
All inputs are finite; a program needn't handle non-finite values.
Results may differ from a plain program's by a relative error of at most 0.0053.
Values may be sent and summed in bfloat16 or wider, within the bound.
A program may use at most 64 MiB of HBM per device.

v0:
```python
import math

import jax
import jax.numpy as jnp
from jax import lax
from jax.sharding import PartitionSpec as P

MODES = 16
STEP = 10


learn_rate = 0.01
beta_first = 0.9
beta_second = 0.95
decay_rate = 0.1
epsilon = 1e-08


def axis_parts(count_xdim):
    freq_list = jnp.arange(MODES, dtype=jnp.int32)
    cell_list = jnp.arange(count_xdim, dtype=jnp.int32)
    phases = (
        jnp.mod(freq_list[:, None] * cell_list[None, :], count_xdim).astype(jnp.float32)
        / count_xdim
    )
    angles = 2.0 * math.pi * phases
    scaling = 1.0 / math.sqrt(count_xdim)
    return (
        (jnp.cos(angles) * scaling).astype(jnp.bfloat16),
        (jnp.sin(angles) * scaling).astype(jnp.bfloat16),
    )


def doubling_table():
    return jnp.where(jnp.arange(MODES, dtype=jnp.int32) > 0, 2.0, 1.0).astype(jnp.float32)


def gelu_slope(values):
    cumulative = 0.5 * (1.0 + lax.erf(values * 0.7071067811865476))
    bell_curve = jnp.exp(-0.5 * values * values) * 0.3989422804014327
    return cumulative + values * bell_curve


def send_pencils(field):
    return lax.all_to_all(field, "dom", split_axis=3, concat_axis=2, tiled=True)


def send_slabs(field):
    return lax.all_to_all(field, "dom", split_axis=2, concat_axis=3, tiled=True)


def forward_parts(field, cosines, sines):
    real_part = jnp.einsum("scxl,fx->slcf", field, cosines, preferred_element_type=jnp.float32)
    imag_part = -jnp.einsum("scxl,fx->slcf", field, sines, preferred_element_type=jnp.float32)
    return (real_part, imag_part)


def inverse_cells(values_real, values_imag, cosines, sines):
    first = jnp.einsum("slcf,fx->scxl", values_real, cosines, preferred_element_type=jnp.float32)
    second = jnp.einsum("slcf,fx->scxl", values_imag, sines, preferred_element_type=jnp.float32)
    return (first - second).astype(jnp.bfloat16)


def on_device(
    density, upstream, spectral_weight, moment_one, moment_two, skip_weight, skip_bias, mode_counts
):
    samples, channels, slab_rows, line_count = density.shape
    count_xdim = slab_rows * lax.axis_size("dom")
    cosines, sines = axis_parts(count_xdim)
    doubling = doubling_table()
    doubling_low = doubling.astype(jnp.bfloat16)
    counts_here = lax.dynamic_slice_in_dim(mode_counts, lax.axis_index("dp") * samples, samples, 0)
    keep_modes = (jnp.arange(MODES, dtype=jnp.int32)[None, :] < counts_here[:, None]).astype(
        jnp.float32
    )
    keep_wide = keep_modes[:, None, None, :]
    weight_short = spectral_weight.astype(jnp.bfloat16)
    group_low = lax.all_gather(weight_short, "dom", axis=0, tiled=True)
    weight_low = lax.all_gather(group_low, "dp", axis=0, tiled=True)
    weight_low = weight_low.reshape(2, MODES, channels, channels)
    weight_real = weight_low[0]
    weight_imag = weight_low[1]
    density_lines = send_pencils(density)
    real_part, imag_part = forward_parts(density_lines, cosines, sines)
    spec_real = real_part.astype(jnp.bfloat16)
    spec_imag = imag_part.astype(jnp.bfloat16)
    form = "slcf,fco->slof"
    mixed_real = jnp.einsum(
        form, spec_real, weight_real, preferred_element_type=jnp.float32
    ) - jnp.einsum(form, spec_imag, weight_imag, preferred_element_type=jnp.float32)
    mixed_imag = jnp.einsum(
        form, spec_imag, weight_real, preferred_element_type=jnp.float32
    ) + jnp.einsum(form, spec_real, weight_imag, preferred_element_type=jnp.float32)
    mixed_real = (mixed_real * keep_wide).astype(jnp.bfloat16) * doubling_low
    mixed_imag = (mixed_imag * keep_wide).astype(jnp.bfloat16) * doubling_low
    back_lines = inverse_cells(mixed_real, mixed_imag, cosines, sines)
    back_rows = send_slabs(back_lines)
    skip_part = jnp.einsum(
        "oc,scxl->soxl", skip_weight, density, preferred_element_type=jnp.float32
    )
    before = back_rows.astype(jnp.float32) + skip_part + skip_bias[None, :, None, None]
    gate_grad = (upstream.astype(jnp.float32) * gelu_slope(before)).astype(jnp.bfloat16)
    gate_lines = send_pencils(gate_grad)
    grad_real, grad_imag = forward_parts(gate_lines, cosines, sines)
    scale = keep_wide * doubling
    grad_real = (grad_real * scale).astype(jnp.bfloat16)
    grad_imag = (grad_imag * scale).astype(jnp.bfloat16)
    outer = "slof,slcf->fco"
    part_real = jnp.einsum(
        outer, grad_real, spec_real, preferred_element_type=jnp.float32
    ) + jnp.einsum(outer, grad_imag, spec_imag, preferred_element_type=jnp.float32)
    part_imag = jnp.einsum(
        outer, grad_imag, spec_real, preferred_element_type=jnp.float32
    ) - jnp.einsum(outer, grad_real, spec_imag, preferred_element_type=jnp.float32)
    grad_local = jnp.stack([part_real, part_imag], 0).reshape(2 * MODES * channels, channels)
    group_grad = lax.psum_scatter(
        grad_local.astype(jnp.bfloat16), "dp", scatter_dimension=0, tiled=True
    ).astype(jnp.float32)
    weight_grad = lax.psum_scatter(group_grad, "dom", scatter_dimension=0, tiled=True)
    inner = "fco,slof->slcf"
    input_real = jnp.einsum(
        inner, weight_real, grad_real, preferred_element_type=jnp.float32
    ) + jnp.einsum(inner, weight_imag, grad_imag, preferred_element_type=jnp.float32)
    input_imag = jnp.einsum(
        inner, weight_real, grad_imag, preferred_element_type=jnp.float32
    ) - jnp.einsum(inner, weight_imag, grad_real, preferred_element_type=jnp.float32)
    input_lines = inverse_cells(
        input_real.astype(jnp.bfloat16), input_imag.astype(jnp.bfloat16), cosines, sines
    )
    input_rows = send_slabs(input_lines)
    skip_back = jnp.einsum(
        "oc,soxl->scxl", skip_weight, gate_grad, preferred_element_type=jnp.float32
    )
    input_grad = (input_rows.astype(jnp.float32) + skip_back).astype(jnp.bfloat16)
    new_moment_one = beta_first * moment_one + (1.0 - beta_first) * weight_grad
    new_moment_two = beta_second * moment_two + (1.0 - beta_second) * weight_grad * weight_grad
    first_hat = new_moment_one / (1.0 - beta_first**STEP)
    second_hat = new_moment_two / (1.0 - beta_second**STEP)
    new_weight = spectral_weight - learn_rate * (
        first_hat / (jnp.sqrt(second_hat) + epsilon) + decay_rate * spectral_weight
    )
    return (input_grad, new_weight, new_moment_one, new_moment_two)


def solution(mesh):
    placed = (
        P("dp", None, "dom", None),
        P("dp", None, "dom", None),
        P(("dp", "dom"), None),
        P(("dp", "dom"), None),
        P(("dp", "dom"), None),
        P(),
        P(),
        P(),
    )
    return jax.shard_map(
        on_device,
        mesh=mesh,
        in_specs=placed,
        out_specs=(
            P("dp", None, "dom", None),
            P(("dp", "dom"), None),
            P(("dp", "dom"), None),
            P(("dp", "dom"), None),
        ),
        check_vma=False,
    )
```

profile of v0, /device:TPU:0, one launch (start us, length us, event | category | flops | bytes accessed | tf_op | source)
XLA Modules:
  0.0 197.6 jit_solution(9866460076303128537)
XLA Ops:
  7.2 1.4 copy.79
  8.6 1.1 reshape.187
  9.7 8.4 %all-to-all-start = ((bf16[16,2,4096]{2,1,0:T(2,128)(2,1)}), bf16[16,2,4096]{2,1,0:T(2,128)(2,1)S(1)}, u32[]{:S(2)}, u32[]{:S(2)}) async-start(bf16[16,2,4096]{2,1,0:T(2,128)(2,1)} %reshape.187), calls=%async_computation | async-start | bytes 524288 | tf_op jit(solution)/shard_map/all_to_all | solution.py:45
  18.2 42.4 %all_gather.6 = bf16[1024,64]{1,0:T(8,128)(2,1)S(1)} all-gather(bf16[64,64]{1,0:T(8,128)(2,1)S(1)} %convert_element_type.194), channel_id=1, replica_groups=mesh['dp'=2,'dom'=16] {'dom'}, dimensions={0}, use_global_device_ids=true | all-gather | bytes 139264 | tf_op jit(solution)/shard_map/all_gather | solution.py:78
  60.6 2.2 %all_gather.7 = bf16[2048,64]{1,0:T(8,128)(2,1)S(1)} all-gather(bf16[1024,64]{1,0:T(8,128)(2,1)S(1)} %all_gather.6), channel_id=1, replica_groups=mesh['dp'=2,'dom'=16] {'dp'}, dimensions={0}, use_global_device_ids=true | all-gather | bytes 393216 | tf_op jit(solution)/shard_map/all_gather | solution.py:79
  62.7 0.7 copy-done.6
  63.4 0.6 dynamic_slice.3
  64.0 0.6 compare_convert_fusion
  64.7 0.3 reshape.188
  65.2 0.5 copy.82
  65.6 0.3 fusion.27
  65.9 0.3 fusion.26
  67.4 0.3 fusion.11
  67.6 0.4 copy.90
  68.1 0.4 reshape.189
  68.5 13.0 %all_to_all.48 = bf16[16,2,4096]{2,1,0:T(2,128)(2,1)S(1)} all-to-all(bf16[16,2,4096]{2,1,0:T(2,128)(2,1)S(1)} %reshape.189), channel_id=1, replica_groups=mesh['dp'=2,'dom'=16] {'dom'}, dimensions={0} | all-to-all | bytes 524288 | tf_op jit(solution)/shard_map/all_to_all | solution.py:49
  81.5 0.3 reshape.190
  82.1 0.3 copy.94
  82.4 0.6 copy-done.1
  83.1 0.4 fusion.41
  83.5 0.3 copy.95
  83.9 1.1 reshape.191
  85.0 3.5 %all-to-all-start.2 = ((bf16[16,2,4096]{2,1,0:T(2,128)(2,1)}), bf16[16,2,4096]{2,1,0:T(2,128)(2,1)S(1)}, u32[]{:S(2)}, u32[]{:S(2)}) async-start(bf16[16,2,4096]{2,1,0:T(2,128)(2,1)} %reshape.191), calls=%async_computation.2 | async-start | bytes 524288 | tf_op jit(solution)/shard_map/all_to_all | solution.py:45
  88.5 0.7 compare_select_fusion.1
  89.2 8.7 %all-to-all-done.2 = bf16[16,2,4096]{2,1,0:T(2,128)(2,1)S(1)} async-done(((bf16[16,2,4096]{2,1,0:T(2,128)(2,1)}), bf16[16,2,4096]{2,1,0:T(2,128)(2,1)S(1)}, u32[]{:S(2)}, u32[]{:S(2)}) %all-to-all-start.2) | async-done | bytes 262176 | tf_op jit(solution)/shard_map/all_to_all | solution.py:45
  97.9 0.3 reshape.192
  98.4 0.5 copy.98
  98.9 0.3 fusion.28
  99.2 0.3 fusion.29
  99.8 0.3 fusion.57
  100.3 0.3 fusion.50
  101.1 0.3 fusion.45
  101.4 0.3 fusion.9
  101.7 0.3 fusion.8
  101.9 0.9 pad_maximum_fusion
  102.9 0.3 fusion.10
  103.2 0.4 copy.106
  103.6 1.1 reshape.193
  104.7 3.5 %all-to-all-start.3 = ((bf16[16,2,4096]{2,1,0:T(2,128)(2,1)}), bf16[16,2,4096]{2,1,0:T(2,128)(2,1)S(1)}, u32[]{:S(2)}, u32[]{:S(2)}) async-start(bf16[16,2,4096]{2,1,0:T(2,128)(2,1)} %reshape.193), calls=%async_computation.3 | async-start | bytes 524288 | tf_op jit(solution)/shard_map/all_to_all | solution.py:49
  108.3 0.6 reduce-scatter.3.cloned.1.call-done
  108.9 1.8 convert_element_type.230
  110.7 6.7 %all-to-all-done.3 = bf16[16,2,4096]{2,1,0:T(2,128)(2,1)S(1)} async-done(((bf16[16,2,4096]{2,1,0:T(2,128)(2,1)}), bf16[16,2,4096]{2,1,0:T(2,128)(2,1)S(1)}, u32[]{:S(2)}, u32[]{:S(2)}) %all-to-all-start.3) | async-done | bytes 262176 | tf_op jit(solution)/shard_map/all_to_all | solution.py:49
  117.5 0.3 reshape.194
  118.0 0.3 copy.110
  118.3 0.3 fusion.3
  118.7 0.9 copy.119
  119.5 69.8 %reduce-scatter.5.cloned.1.call-done = f32[64,64]{1,0:T(8,128)} async-done(((f32[1024,64]{1,0:T(8,128)}), f32[64,64]{1,0:T(8,128)}) %reduce-scatter.5.cloned.1.call-update) | async-done | bytes 16400 | tf_op jit(solution)/shard_map/reduce_scatter | solution.py:119
  189.4 1.4 multiply_subtract_fusion
  (39 shorter events, 3.0 us)
Async XLA Ops:
  7.2 75.3 %copy-start = (bf16[64,64]{1,0:T(8,128)(2,1)S(1)}, bf16[64,64]{1,0:T(8,128)(2,1)}, u32[]{:S(2)}) copy-start(bf16[64,64]{1,0:T(8,128)(2,1)} %param.13) | copy-start | bytes 24580
  9.7 8.5 %copy-start.2 = (f32[64,64]{1,0:T(8,128)S(1)}, f32[64,64]{1,0:T(8,128)}, u32[]{:S(2)}) copy-start(f32[64,64]{1,0:T(8,128)} %param.10) | copy-start | bytes 49156
  9.7 55.0 %all-to-all-start = ((bf16[16,2,4096]{2,1,0:T(2,128)(2,1)}), bf16[16,2,4096]{2,1,0:T(2,128)(2,1)S(1)}, u32[]{:S(2)}, u32[]{:S(2)}) async-start(bf16[16,2,4096]{2,1,0:T(2,128)(2,1)} %reshape.187), calls=%async_computation | async-start | bytes 524288 | tf_op jit(solution)/shard_map/all_to_all | solution.py:45
  62.7 0.7 copy-start.6
  82.1 1.0 copy-start.1
  82.1 1.0 copy-start.5
  82.4 0.7 copy-start.7
  85.0 13.0 %all-to-all-start.2 = ((bf16[16,2,4096]{2,1,0:T(2,128)(2,1)}), bf16[16,2,4096]{2,1,0:T(2,128)(2,1)S(1)}, u32[]{:S(2)}, u32[]{:S(2)}) async-start(bf16[16,2,4096]{2,1,0:T(2,128)(2,1)} %reshape.191), calls=%async_computation.2 | async-start | bytes 524288 | tf_op jit(solution)/shard_map/all_to_all | solution.py:45
  88.5 20.4 %reduce-scatter.3.cloned.1.call-start = ((), (), s32[]{:S(2)}) async-start(), calls=%async_computation.6 | async-start | bytes 786432 | tf_op jit(solution)/shard_map/reduce_scatter | solution.py:116
  104.7 12.8 %all-to-all-start.3 = ((bf16[16,2,4096]{2,1,0:T(2,128)(2,1)}), bf16[16,2,4096]{2,1,0:T(2,128)(2,1)S(1)}, u32[]{:S(2)}, u32[]{:S(2)}) async-start(bf16[16,2,4096]{2,1,0:T(2,128)(2,1)} %reshape.193), calls=%async_computation.3 | async-start | bytes 524288 | tf_op jit(solution)/shard_map/all_to_all | solution.py:49
  108.3 81.1 %reduce-scatter.5.cloned.1.call-start = ((), (), s32[]{:S(2)}) async-start(), calls=%async_computation.7 | async-start | bytes 557056 | tf_op jit(solution)/shard_map/reduce_scatter | solution.py:119
  118.6 70.7 %copy-start.3 = (f32[64,64]{1,0:T(8,128)S(1)}, f32[64,64]{1,0:T(8,128)}, u32[]{:S(2)}) copy-start(f32[64,64]{1,0:T(8,128)} %param.11) | copy-start | bytes 49156
  118.6 70.7 %copy-start.4 = (f32[64,64]{1,0:T(8,128)S(1)}, f32[64,64]{1,0:T(8,128)}, u32[]{:S(2)}) copy-start(f32[64,64]{1,0:T(8,128)} %param.12) | copy-start | bytes 49156
Sparse Core Ops, SparseCore 0:
  103.0 5.8 reduce-scatter.2
  111.4 77.8 reduce-scatter.4
where the time goes:
time: 198 us
  waiting for transfers between devices  85.9 us (43%)
  blocking collectives  57.6 us (29%)
  starting transfers between devices  15.6 us (8%)
  between operations  14.4 us (7%)
  local copies, waits for them, and re-layouts  12.5 us (6%)
  matrix products  5.96 us (3%)
  other arithmetic  5.61 us (3%)
    reduce_scatter x1, waiting for transfers between devices, on_device(): lax.psum_scatter(group_grad, 'dom', scatter_dimension=0, tiled=True)  69.8 us
    all_gather x1, blocking collectives, on_device(): group_low = lax.all_gather(weight_short, 'dom', axis=0, tiled=True)  42.4 us
    all_to_all x1, blocking collectives, send_slabs(): return lax.all_to_all(field, 'dom', split_axis=2, concat_axis=3, tiled=True)  13 us
    all_to_all x2, starting transfers between devices, send_pencils(): return lax.all_to_all(field, 'dom', split_axis=3, concat_axis=2, tiled=True)  12 us
    unnamed x26, local copies, waits for them, and re-layouts  8.74 us
    all_to_all x2, waiting for transfers between devices, send_pencils(): return lax.all_to_all(field, 'dom', split_axis=3, concat_axis=2, tiled=True)  8.72 us
    all_to_all x1, waiting for transfers between devices, send_slabs(): return lax.all_to_all(field, 'dom', split_axis=2, concat_axis=3, tiled=True)  6.75 us
  transfers between devices with their start and end apart: 5, of which 4 were waited for; matrix products, arithmetic and copies ran while one was open for 4% of the time, Pallas kernels for 0%

commit v1 on v0

--- a/solution.py
+++ b/solution.py
@@ -1,8 +1,12 @@
+import functools
 import math
 
 import jax
 import jax.numpy as jnp
+import numpy as np
 from jax import lax
+from jax.experimental import pallas as pl
+from jax.experimental.pallas import tpu as pltpu
 from jax.sharding import PartitionSpec as P
 
 MODES = 16
@@ -142,6 +146,389 @@
     return (input_grad, new_weight, new_moment_one, new_moment_two)
 
 
+MESH = pl.DeviceIdType.MESH
+ROWS = 8
+STREAMS = 2
+
+
+def fixed_tables(devices, own, rows):
+    cells = devices * rows
+    freq = np.arange(MODES)[:, None]
+    angles = 2.0 * np.pi * ((freq * np.arange(cells)[None, :]) % cells) / cells
+    scaling = 1.0 / math.sqrt(cells)
+    parts = np.stack([np.cos(angles) * scaling, -np.sin(angles) * scaling], 1)
+    parts = parts.reshape(MODES, 2, 1, devices, 1, rows)
+    same = np.eye(own).reshape(1, 1, own, 1, own, 1)
+    transform = (parts * same).reshape(MODES * 2 * own, devices * own * rows)
+    channels = devices * own
+    order = np.zeros((2, devices, own, devices, 2, own))
+    for part in range(2):
+        for device in range(devices):
+            for one in range(own):
+                order[part, device, one, device, part, one] = 1.0
+    order = order.reshape(2 * channels, 2 * channels)
+    spread = np.repeat(np.eye(channels), rows, axis=0)
+    low = lambda table: jnp.asarray(table.astype(np.float32), jnp.bfloat16)
+    return low(transform), low(transform.T), low(order), low(order.T), low(spread)
+
+
+def dot(left, right, dims=((1,), (0,))):
+    return lax.dot_general(left, right, (dims, ((), ())), preferred_element_type=jnp.float32)
+
+
+def step_kernel(
+    n,
+    dens,
+    upst,
+    weight,
+    first,
+    second,
+    skip,
+    bias,
+    counts,
+    trans,
+    trans_back,
+    order,
+    order_back,
+    spread,
+    out,
+    new_weight,
+    new_first,
+    new_second,
+    a1r,
+    a2s,
+    a2r,
+    b1s,
+    b1r,
+    b2s,
+    b2r,
+    c1s,
+    c1r,
+    c2s,
+    c2r,
+    d1s,
+    d1r,
+    d2s,
+    d2r,
+    skip_part,
+    kept,
+    wsend,
+    wrecv,
+    gsend,
+    grecv,
+    send_sem,
+    recv_sem,
+    pair_send,
+    pair_recv,
+):
+    me = lax.axis_index("dom")
+    core = lax.axis_index("dp")
+    low, wide = jnp.bfloat16, jnp.float32
+    block = dens.shape[0] // n
+    width = dens.shape[1] // STREAMS
+    channels = weight.shape[0]
+
+    barrier = pltpu.get_barrier_semaphore()
+
+    def greet(shift, carry):
+        pl.semaphore_signal(
+            barrier, inc=1, device_id=(core, lax.rem(me + shift, n)), device_id_type=MESH
+        )
+        return carry
+
+    lax.fori_loop(1, n, greet, 0)
+    pl.semaphore_signal(barrier, inc=1, device_id=(1 - core, me), device_id_type=MESH)
+    pl.semaphore_wait(barrier, n)
+
+    def remote(stage, stream, shift, source, target):
+        return pltpu.make_async_remote_copy(
+            src_ref=source,
+            dst_ref=target,
+            send_sem=send_sem.at[stage, stream, shift],
+            recv_sem=recv_sem.at[stage, stream, shift],
+            device_id=(core, lax.rem(me + shift, n)),
+            device_id_type=MESH,
+        )
+
+    def send_all(stage, stream, source, target):
+        def one(shift, carry):
+            peer = lax.rem(me + shift, n)
+            remote(stage, stream, shift, source.at[stream, peer], target.at[stream, me]).start()
+            return carry
+
+        lax.fori_loop(1, n, one, 0)
+        target[stream, me] = source[stream, me]
+
+    def wait_all(stage, stream, source, target):
+        def one(shift, carry):
+            remote(stage, stream, shift, source.at[stream, me], target.at[stream, me]).wait_recv()
+            return carry
+
+        lax.fori_loop(1, n, one, 0)
+
+    def lanes(stream):
+        return pl.ds(stream * width, width)
+
+    def rows(device):
+        return pl.ds(pl.multiple_of(device * block, block), block)
+
+    for stream in range(STREAMS):
+
+        def start_one(shift, carry):
+            peer = lax.rem(me + shift, n)
+            remote(
+                0, stream, shift, dens.at[rows(peer), lanes(stream)], a1r.at[stream, me]
+            ).start()
+            return carry
+
+        lax.fori_loop(1, n, start_one, 0)
+        a1r[stream, me] = dens[rows(me), lanes(stream)]
+
+    own_low = weight[...].astype(low)
+    wsend[...] = jnp.concatenate([own_low, own_low], axis=1)
+    swap = pltpu.make_async_remote_copy(
+        src_ref=wsend,
+        dst_ref=wrecv,
+        send_sem=pair_send.at[0],
+        recv_sem=pair_recv.at[0],
+        device_id=(1 - core, me),
+        device_id_type=MESH,
+    )
+    swap.start()
+
+    size = dens.shape[0]
+    same_row = lax.rem(lax.broadcasted_iota(jnp.int32, (size, size), 0), ROWS) == lax.rem(
+        lax.broadcasted_iota(jnp.int32, (size, size), 1), ROWS
+    )
+    spread_low = spread[...]
+
+    def wide_map(dims):
+        tall = dot(spread_low, skip[...], dims).astype(low)
+        full = dot(tall, spread_low, ((1,), (1,)))
+        return jnp.where(same_row, full, 0.0).astype(low)
+
+    skip_part[...] = dot(wide_map(((1,), (0,))), dens[...]) + bias[...]
+    back_map = wide_map(((1,), (1,)))
+
+    swap.wait_recv()
+    mine = weight[...].astype(low).astype(wide)
+    other = wrecv[...].astype(wide)[:, :channels]
+    is_first = core == 0
+    weight_real = jnp.where(is_first, mine, other)
+    weight_imag = jnp.where(is_first, other, mine)
+    mixer = jnp.concatenate(
+        [
+            jnp.concatenate([weight_real, weight_imag], axis=1),
+            jnp.concatenate([-weight_imag, weight_real], axis=1),
+        ],
+        axis=0,
+    )
+    mixer_back = mixer.T.astype(low)
+    mixer = mixer.astype(low)
+    keep = jnp.where(me < counts[core], 1.0, 0.0)
+    scale = keep * jnp.where(me == 0, 1.0, 2.0)
+
+    def by_device(values):
+        return values.reshape(n, values.shape[0] // n, values.shape[1])
+
+    def flat(ref, stream):
+        values = ref[stream]
+        return values.reshape(values.shape[0] * values.shape[1], values.shape[2])
+
+    for stream in range(STREAMS):
+        wait_all(0, stream, a1r, a1r)
+        a2s[stream] = by_device(dot(trans[...], flat(a1r, stream)))
+        send_all(1, stream, a2s, a2r)
+    for stream in range(STREAMS):
+        wait_all(1, stream, a2s, a2r)
+        spectrum = dot(order[...], flat(a2r, stream).astype(low)).astype(low)
+        kept[stream] = spectrum
+        mixed = (dot(mixer_back, spectrum) * scale).astype(low)
+        b1s[stream] = by_device(dot(order_back[...], mixed))
+        send_all(2, stream, b1s, b1r)
+    for stream in range(STREAMS):
+        wait_all(2, stream, b1s, b1r)
+        b2s[stream] = by_device(dot(trans_back[...], flat(b1r, stream).astype(low)).astype(low))
+        send_all(3, stream, b2s, b2r)
+    for stream in range(STREAMS):
+
+        def slope_block(device):
+            before = b2r[stream, device].astype(wide) + skip_part[rows(device), lanes(stream)]
+            cotangent = upst[rows(device), lanes(stream)].astype(wide)
+            c1s[stream, device] = (cotangent * gelu_slope(before)).astype(low)
+
+        slope_block(me)
+        c1r[stream, me] = c1s[stream, me]
+
+        def one_slope(step, carry):
+            shift = n - step
+            device = lax.rem(me + step, n)
+            remote(3, stream, shift, b2s.at[stream, me], b2r.at[stream, me]).wait_recv()
+            slope_block(device)
+            remote(4, stream, step, c1s.at[stream, device], c1r.at[stream, me]).start()
+            return carry
+
+        lax.fori_loop(1, n, one_slope, 0)
+    for stream in range(STREAMS):
+        wait_all(4, stream, c1s, c1r)
+        c2s[stream] = by_device(dot(trans[...], flat(c1r, stream)))
+        send_all(5, stream, c2s, c2r)
+    products = jnp.zeros((2 * channels, 2 * channels), wide)
+    for stream in range(STREAMS):
+        wait_all(5, stream, c2s, c2r)
+        gradient = (dot(order[...], flat(c2r, stream).astype(low)) * scale).astype(low)
+        returned = dot(mixer, gradient).astype(low)
+        d1s[stream] = by_device(dot(order_back[...], returned))
+        send_all(6, stream, d1s, d1r)
+        products += dot(kept[stream], gradient, ((1,), (1,)))
+    top, bottom = products[:channels], products[channels:]
+    grad_real = top[:, :channels] + bottom[:, channels:]
+    grad_imag = top[:, channels:] - bottom[:, :channels]
+    theirs = jnp.where(is_first, grad_imag, grad_real)
+    ours = jnp.where(is_first, grad_real, grad_imag)
+    gsend[...] = jnp.concatenate([theirs, theirs], axis=1)
+    swap_grad = pltpu.make_async_remote_copy(
+        src_ref=gsend,
+        dst_ref=grecv,
+        send_sem=pair_send.at[1],
+        recv_sem=pair_recv.at[1],
+        device_id=(1 - core, me),
+        device_id_type=MESH,
+    )
+    swap_grad.start()
+    for stream in range(STREAMS):
+        wait_all(6, stream, d1s, d1r)
+        d2s[stream] = by_device(dot(trans_back[...], flat(d1r, stream).astype(low)).astype(low))
+        send_all(7, stream, d2s, d2r)
+    for stream in range(STREAMS):
+        skip_part[:, lanes(stream)] = dot(back_map, flat(c1s, stream))
+    swap_grad.wait_recv()
+    weight_grad = ours + grecv[...][:, :channels]
+    one = beta_first * first[...] + (1.0 - beta_first) * weight_grad
+    two = beta_second * second[...] + (1.0 - beta_second) * weight_grad * weight_grad
+    new_first[...] = one
+    new_second[...] = two
+    first_hat = one / (1.0 - beta_first**STEP)
+    second_hat = two / (1.0 - beta_second**STEP)
+    new_weight[...] = weight[...] - learn_rate * (
+        first_hat / (jnp.sqrt(second_hat) + epsilon) + decay_rate * weight[...]
+    )
+    for stream in range(STREAMS):
+
+        def final_block(device):
+            total = d2r[stream, device].astype(wide) + skip_part[rows(device), lanes(stream)]
+            out[rows(device), lanes(stream)] = total.astype(low)
+
+        final_block(me)
+
+        def one_final(step, carry):
+            shift = n - step
+            remote(7, stream, shift, d2s.at[stream, me], d2r.at[stream, me]).wait_recv()
+            final_block(lax.rem(me + step, n))
+            return carry
+
+        lax.fori_loop(1, n, one_final, 0)
+
+    swap.wait_send()
+    swap_grad.wait_send()
+    sources = (a1r, a2s, b1s, b2s, c1s, c2s, d1s, d2s)
+    for stage, source in enumerate(sources):
+        for stream in range(STREAMS):
+
+            def sent(shift, carry):
+                remote(
+                    stage, stream, shift, source.at[stream, me], source.at[stream, me]
+                ).wait_send()
+                return carry
+
+            lax.fori_loop(1, n, sent, 0)
+
+
+def one_frequency_each(
+    n, density, upstream, spectral_weight, moment_one, moment_two, skip_weight, skip_bias, mode_counts
+):
+    samples, channels, slab_rows, line_count = density.shape
+    own = channels // n
+    width = line_count // STREAMS
+    size = channels * slab_rows
+    tables = fixed_tables(n, own, slab_rows)
+    low, wide = jnp.bfloat16, jnp.float32
+    vmem = pl.BlockSpec(memory_space=pltpu.VMEM)
+    cells = pltpu.VMEM((STREAMS, n, own * slab_rows, width), low)
+    modes = pltpu.VMEM((STREAMS, n, 2 * own, width), wide)
+    result = pl.pallas_call(
+        functools.partial(step_kernel, n),
+        out_shape=(
+            jax.ShapeDtypeStruct((size, line_count), low),
+            jax.ShapeDtypeStruct((channels, channels), wide),
+            jax.ShapeDtypeStruct((channels, channels), wide),
+            jax.ShapeDtypeStruct((channels, channels), wide),
+        ),
+        in_specs=[vmem] * 7 + [pl.BlockSpec(memory_space=pltpu.SMEM)] + [vmem] * 5,
+        out_specs=(vmem,) * 4,
+        scratch_shapes=[
+            cells,
+            modes,
+            modes,
+            modes,
+            modes,
+            cells,
+            cells,
+            cells,
+            cells,
+            modes,
+            modes,
+            modes,
+            modes,
+            cells,
+            cells,
+            pltpu.VMEM((size, line_count), wide),
+            pltpu.VMEM((STREAMS, 2 * channels, width), low),
+            pltpu.VMEM((channels, 2 * channels), low),
+            pltpu.VMEM((channels, 2 * channels), low),
+            pltpu.VMEM((channels, 2 * channels), wide),
+            pltpu.VMEM((channels, 2 * channels), wide),
+            pltpu.SemaphoreType.DMA((8, STREAMS, n)),
+            pltpu.SemaphoreType.DMA((8, STREAMS, n)),
+            pltpu.SemaphoreType.DMA((2,)),
+            pltpu.SemaphoreType.DMA((2,)),
+        ],
+        compiler_params=pltpu.CompilerParams(
+            collective_id=0, has_side_effects=True, vmem_limit_bytes=40 * 1024 * 1024
+        ),
+        cost_estimate=pl.CostEstimate(
+            flops=1_000_000_000, bytes_accessed=2_000_000, transcendentals=300_000
+        ),
+    )(
+        density.reshape(size, line_count),
+        upstream.reshape(size, line_count),
+        spectral_weight,
+        moment_one,
+        moment_two,
+        skip_weight,
+        jnp.repeat(skip_bias, slab_rows)[:, None],
+        mode_counts,
+        *tables,
+    )
+    return (result[0].reshape(density.shape), *result[1:])
+
+
+def on_mesh(density, *others):
+    samples, channels, slab_rows, line_count = density.shape
+    n, groups = lax.axis_size("dom"), lax.axis_size("dp")
+    fits = (
+        n == MODES
+        and groups == 2
+        and samples == 1
+        and slab_rows == ROWS
+        and 2 * (channels // n) == 8
+        and line_count % (128 * STREAMS) == 0
+    )
+    if fits:
+        return one_frequency_each(n, density, *others)
+    return on_device(density, *others)
+
+
 def solution(mesh):
     placed = (
         P("dp", None, "dom", None),
@@ -154,7 +541,7 @@
         P(),
     )
     return jax.shard_map(
-        on_device,
+        on_mesh,
         mesh=mesh,
         in_specs=placed,
         out_specs=(

time: 198 us -> 71.3 us (0.36)
  waiting for transfers between devices: 85.9 us -> 0 us
  Pallas kernels: 0 us -> 59.4 us
  blocking collectives: 57.6 us -> 0 us
  starting transfers between devices: 15.6 us -> 0 us
  between operations: 14.4 us -> 0.68 us
  matrix products: 5.96 us -> 0 us
  other arithmetic: 5.61 us -> 0 us
    reduce_scatter x2 -> x0, waiting for transfers between devices: 70.4 us -> none  [the longest x1 69.8 us: on_device(): lax.psum_scatter(group_grad, 'dom', scatter_dimension=0, tiled=True)]
    pallas_call x0 -> x1, Pallas kernels: none -> 59.4 us  [one_frequency_each(): pl.pallas_call(functools.partial(step_kernel, n), out_shape=(jax.ShapeDty...]
    all_gather x2 -> x0, blocking collectives: 44.5 us -> none  [the longest x1 42.4 us: on_device(): group_low = lax.all_gather(weight_short, 'dom', axis=0, tiled=True)]
    all_to_all x3 -> x0, starting transfers between devices: 15.5 us -> none  [the longest x2 12 us: send_pencils(): return lax.all_to_all(field, 'dom', split_axis=3, concat_axis=2, tiled=True)]
    all_to_all x3 -> x0, waiting for transfers between devices: 15.5 us -> none  [the longest x2 8.72 us: send_pencils(): return lax.all_to_all(field, 'dom', split_axis=3, concat_axis=2, tiled=True)]
    all_to_all x1 -> x0, blocking collectives: 13 us -> none  [send_slabs(): return lax.all_to_all(field, 'dom', split_axis=2, concat_axis=3, tiled=True)]
    dot_general x22 -> x0, matrix products: 5.96 us -> none  [the longest x2 0.65 us: forward_parts(): jnp.einsum('scxl,fx->slcf', field, cosines, preferred_element_type=jnp.fl...]
    convert_element_type x6 -> x0, other arithmetic: 2.64 us -> none  [the longest x1 1.78 us: on_device(): group_grad = lax.psum_scatter(grad_local.astype(jnp.bfloat16), 'dp', scat...]
  transfers between devices with their start and end apart: 5 -> 0, of which waited for: 4 -> 0; matrix products, arithmetic and copies ran while one was open for 4% -> 0% of each run, Pallas kernels for 0% -> 0%
where the time goes in v1:
time: 71.3 us; the launch traced here: 70.8 us
  Pallas kernels  59.4 us (83%)
  local copies, waits for them, and re-layouts  10.8 us (15%)
    pallas_call x1, Pallas kernels, one_frequency_each(): pl.pallas_call(functools.partial(step_kernel, n), out_shape=(jax.ShapeDty...  59.4 us
    unnamed x28, local copies, waits for them, and re-layouts  9.86 us

profile of v1, /device:TPU:0, one launch (start us, length us, event | category | flops | bytes accessed | tf_op | source)
XLA Modules:
  0.0 70.8 jit_solution(14157897414799123715)
XLA Ops:
  0.6 0.0 copy-start
  0.6 0.8 %broadcast_in_dim.3 = f32[64,8]{1,0:T(8,128)S(1)} broadcast(f32[64]{0:T(128)} %param.19), dimensions={0} | broadcast | bytes 2304 | tf_op jit(solution)/shard_map/broadcast_in_dim | solution.py:509
  1.4 0.0 copy-start.2
  1.4 0.0 copy-start.3
  1.4 0.0 copy-start.6
  1.4 0.1 broadcast_in_dim_reshape.4.bias
  1.6 0.0 copy-done
  1.6 0.6 copy-done.2
  2.2 0.0 copy-done.3
  2.2 0.0 copy-done.6
  2.2 0.0 copy-start.1
  2.2 0.9 %copy-done.1 = bf16[1,64,8,256]{3,2,1,0:T(8,128)(2,1)S(1)} copy-done((bf16[1,64,8,256]{3,2,1,0:T(8,128)(2,1)S(1)}, bf16[1,64,8,256]{3,2,1,0:T(8,128)(2,1)}, u32[]{:S(2)}) %copy-start.1) | copy-done | bytes 262168
  3.2 0.0 copy-start.4
  3.2 0.8 %copy-done.4 = f32[64,64]{1,0:T(8,128)S(1)} copy-done((f32[64,64]{1,0:T(8,128)S(1)}, f32[64,64]{1,0:T(8,128)}, u32[]{:S(2)}) %copy-start.4) | copy-done | bytes 16408
  3.9 0.0 copy-start.5
  3.9 0.7 %copy-done.5 = bf16[64,64]{1,0:T(8,128)(2,1)S(1)} copy-done((bf16[64,64]{1,0:T(8,128)(2,1)S(1)}, bf16[64,64]{1,0:T(8,128)(2,1)}, u32[]{:S(2)}) %copy-start.5) | copy-done | bytes 8216
  4.6 0.0 copy-start.7
  4.6 0.9 %copy-done.7 = bf16[512,64]{1,0:T(8,128)(2,1)S(1)} copy-done((bf16[512,64]{1,0:T(8,128)(2,1)S(1)}, bf16[512,64]{1,0:T(8,128)(2,1)}, u32[]{:S(2)}) %copy-start.7) | copy-done | bytes 65560
  5.5 0.0 copy-start.8
  5.5 0.9 %copy-done.8 = bf16[512,128]{1,0:T(8,128)(2,1)S(1)} copy-done((bf16[512,128]{1,0:T(8,128)(2,1)S(1)}, bf16[512,128]{1,0:T(8,128)(2,1)}, u32[]{:S(2)}) %copy-start.8) | copy-done | bytes 131096
  6.4 0.0 copy-start.9
  6.4 0.9 %copy-done.9 = bf16[128,512]{1,0:T(8,128)(2,1)S(1)} copy-done((bf16[128,512]{1,0:T(8,128)(2,1)S(1)}, bf16[128,512]{1,0:T(8,128)(2,1)}, u32[]{:S(2)}) %copy-start.9) | copy-done | bytes 131096
  7.4 0.0 copy-start.10
  7.4 0.8 %copy-done.10 = bf16[128,128]{1,0:T(8,128)(2,1)S(1)} copy-done((bf16[128,128]{1,0:T(8,128)(2,1)S(1)}, bf16[128,128]{1,0:T(8,128)(2,1)}, u32[]{:S(2)}) %copy-start.10) | copy-done | bytes 32792
  8.1 0.0 copy-start.11
  8.1 0.8 %copy-done.11 = bf16[128,128]{1,0:T(8,128)(2,1)S(1)} copy-done((bf16[128,128]{1,0:T(8,128)(2,1)S(1)}, bf16[128,128]{1,0:T(8,128)(2,1)}, u32[]{:S(2)}) %copy-start.11) | copy-done | bytes 32792
  8.9 59.4 %shard_map.156 = (bf16[512,256]{1,0:T(8,128)(2,1)S(1)}, f32[64,64]{1,0:T(8,128)S(1)}, f32[64,64]{1,0:T(8,128)S(1)}, f32[64,64]{1,0:T(8,128)S(1)}) custom-call(bf16[512,256]{1,0:T(8,128)(2,1)S(1)} %bitcast.4, bf16[512,256]{1,0:T(8,128)(2,1)S(1)} %bitcast.5, f32[64,64]{1,0:T(8,128)S(1)} %copy-done.2, f32[64,64]{1,0:T(8,128)S(1)} %copy-done.3, ...), custom_call_target="tpu_custom_call" | custom-call | flops 1000000000 | bytes 2000000 | tf_op jit(solution)/shard_map/pallas_call | solution.py:459
  68.2 0.7 copy.22
  68.9 0.6 copy.23
  69.6 0.6 copy.24
  70.2 0.6 copy.25
Async XLA Ops:
  0.6 1.0 %copy-start = (bf16[1,64,8,256]{3,2,1,0:T(8,128)(2,1)S(1)}, bf16[1,64,8,256]{3,2,1,0:T(8,128)(2,1)}, u32[]{:S(2)}) copy-start(bf16[1,64,8,256]{3,2,1,0:T(8,128)(2,1)} %param.13) | copy-start | bytes 786436
  1.4 0.8 %copy-start.2 = (f32[64,64]{1,0:T(8,128)S(1)}, f32[64,64]{1,0:T(8,128)}, u32[]{:S(2)}) copy-start(f32[64,64]{1,0:T(8,128)} %weight.1) | copy-start | bytes 49156
  1.4 0.8 %copy-start.3 = (f32[64,64]{1,0:T(8,128)S(1)}, f32[64,64]{1,0:T(8,128)}, u32[]{:S(2)}) copy-start(f32[64,64]{1,0:T(8,128)} %first.1) | copy-start | bytes 49156
  1.4 0.8 %copy-start.6 = (s32[2]{0:T(128)S(1)}, s32[2]{0:T(128)}, u32[]{:S(2)}) copy-start(s32[2]{0:T(128)} %counts.1) | copy-start | bytes 28
  2.2 1.0 %copy-start.1 = (bf16[1,64,8,256]{3,2,1,0:T(8,128)(2,1)S(1)}, bf16[1,64,8,256]{3,2,1,0:T(8,128)(2,1)}, u32[]{:S(2)}) copy-start(bf16[1,64,8,256]{3,2,1,0:T(8,128)(2,1)} %param.14) | copy-start | bytes 786436
  3.2 0.8 %copy-start.4 = (f32[64,64]{1,0:T(8,128)S(1)}, f32[64,64]{1,0:T(8,128)}, u32[]{:S(2)}) copy-start(f32[64,64]{1,0:T(8,128)} %second.1) | copy-start | bytes 49156
  3.9 0.7 %copy-start.5 = (bf16[64,64]{1,0:T(8,128)(2,1)S(1)}, bf16[64,64]{1,0:T(8,128)(2,1)}, u32[]{:S(2)}) copy-start(bf16[64,64]{1,0:T(8,128)(2,1)} %skip.1) | copy-start | bytes 24580
  4.6 0.9 %copy-start.7 = (bf16[512,64]{1,0:T(8,128)(2,1)S(1)}, bf16[512,64]{1,0:T(8,128)(2,1)}, u32[]{:S(2)}) copy-start(bf16[512,64]{1,0:T(8,128)(2,1)} %constant.14.clone.spread) | copy-start | bytes 196612
  5.5 0.9 %copy-start.8 = (bf16[512,128]{1,0:T(8,128)(2,1)S(1)}, bf16[512,128]{1,0:T(8,128)(2,1)}, u32[]{:S(2)}) copy-start(bf16[512,128]{1,0:T(8,128)(2,1)} %constant.11.clone.trans_back) | copy-start | bytes 393220
  6.4 0.9 %copy-start.9 = (bf16[128,512]{1,0:T(8,128)(2,1)S(1)}, bf16[128,512]{1,0:T(8,128)(2,1)}, u32[]{:S(2)}) copy-start(bf16[128,512]{1,0:T(8,128)(2,1)} %constant.10.clone.trans) | copy-start | bytes 393220
  7.4 0.8 %copy-start.10 = (bf16[128,128]{1,0:T(8,128)(2,1)S(1)}, bf16[128,128]{1,0:T(8,128)(2,1)}, u32[]{:S(2)}) copy-start(bf16[128,128]{1,0:T(8,128)(2,1)} %constant.13.clone.order_back) | copy-start | bytes 98308
  8.1 0.8 %copy-start.11 = (bf16[128,128]{1,0:T(8,128)(2,1)S(1)}, bf16[128,128]{1,0:T(8,128)(2,1)}, u32[]{:S(2)}) copy-start(bf16[128,128]{1,0:T(8,128)(2,1)} %constant.12.clone.order) | copy-start | bytes 98308

commit v2 on v1

--- a/solution.py
+++ b/solution.py
@@ -169,7 +169,7 @@
     order = order.reshape(2 * channels, 2 * channels)
     spread = np.repeat(np.eye(channels), rows, axis=0)
     low = lambda table: jnp.asarray(table.astype(np.float32), jnp.bfloat16)
-    return low(transform), low(transform.T), low(order), low(order.T), low(spread)
+    return low(transform.T), low(order), low(order.T), low(spread)
 
 
 def dot(left, right, dims=((1,), (0,))):
@@ -178,23 +178,28 @@
 
 def step_kernel(
     n,
+    dens_hbm,
+    upst_hbm,
+    weight_hbm,
+    skip_hbm,
+    bias_hbm,
+    counts,
+    trans_back_hbm,
+    order_hbm,
+    order_back_hbm,
+    spread_hbm,
+    out,
+    out_grad,
     dens,
     upst,
     weight,
-    first,
-    second,
     skip,
     bias,
-    counts,
-    trans,
     trans_back,
     order,
     order_back,
     spread,
-    out,
-    new_weight,
-    new_first,
-    new_second,
+    trans,
     a1r,
     a2s,
     a2r,
@@ -218,8 +223,10 @@
     grecv,
     send_sem,
     recv_sem,
+    block_sem,
     pair_send,
     pair_recv,
+    load_sem,
 ):
     me = lax.axis_index("dom")
     core = lax.axis_index("dp")
@@ -228,6 +235,25 @@
     width = dens.shape[1] // STREAMS
     channels = weight.shape[0]
 
+    loads = [
+        pltpu.make_async_copy(source, target, load_sem.at[index])
+        for index, (source, target) in enumerate(
+            (
+                (dens_hbm, dens),
+                (weight_hbm, weight),
+                (skip_hbm, skip),
+                (spread_hbm, spread),
+                (bias_hbm, bias),
+                (order_hbm, order),
+                (order_back_hbm, order_back),
+                (trans_back_hbm, trans_back),
+                (upst_hbm, upst),
+            )
+        )
+    ]
+    for load in loads:
+        load.start()
+
     barrier = pltpu.get_barrier_semaphore()
 
     def greet(shift, carry):
@@ -236,16 +262,17 @@
         )
         return carry
 
-    lax.fori_loop(1, n, greet, 0)
+    lax.fori_loop(1, n, greet, 0, unroll=True)
     pl.semaphore_signal(barrier, inc=1, device_id=(1 - core, me), device_id_type=MESH)
     pl.semaphore_wait(barrier, n)
-
-    def remote(stage, stream, shift, source, target):
+    loads[0].wait()
+
+    def remote(stage, stream, shift, source, target, arrival=None):
         return pltpu.make_async_remote_copy(
             src_ref=source,
             dst_ref=target,
-            send_sem=send_sem.at[stage, stream, shift],
-            recv_sem=recv_sem.at[stage, stream, shift],
+            send_sem=send_sem.at[stage, stream],
+            recv_sem=recv_sem.at[stage, stream] if arrival is None else arrival,
             device_id=(core, lax.rem(me + shift, n)),
             device_id_type=MESH,
         )
@@ -256,15 +283,27 @@
             remote(stage, stream, shift, source.at[stream, peer], target.at[stream, me]).start()
             return carry
 
-        lax.fori_loop(1, n, one, 0)
+        lax.fori_loop(1, n, one, 0, unroll=True)
         target[stream, me] = source[stream, me]
 
-    def wait_all(stage, stream, source, target):
+    def send_blocks(stage, stream, source, target):
         def one(shift, carry):
-            remote(stage, stream, shift, source.at[stream, me], target.at[stream, me]).wait_recv()
+            peer = lax.rem(me + shift, n)
+            remote(
+                stage,
+                stream,
+                shift,
+                source.at[stream, peer],
+                target.at[stream, me],
+                block_sem.at[stage // 4, stream, shift],
+            ).start()
             return carry
 
-        lax.fori_loop(1, n, one, 0)
+        lax.fori_loop(1, n, one, 0, unroll=True)
+
+    def all_of(stage, stream, ref):
+        blocks = ref.at[stream, pl.ds(0, n - 1)]
+        return remote(stage, stream, 1, blocks, blocks)
 
     def lanes(stream):
         return pl.ds(stream * width, width)
@@ -281,9 +320,10 @@
             ).start()
             return carry
 
-        lax.fori_loop(1, n, start_one, 0)
+        lax.fori_loop(1, n, start_one, 0, unroll=True)
         a1r[stream, me] = dens[rows(me), lanes(stream)]
 
+    loads[1].wait()
     own_low = weight[...].astype(low)
     wsend[...] = jnp.concatenate([own_low, own_low], axis=1)
     swap = pltpu.make_async_remote_copy(
@@ -295,21 +335,21 @@
         device_id_type=MESH,
     )
     swap.start()
+    for load in loads[2:]:
+        load.wait()
 
     size = dens.shape[0]
-    same_row = lax.rem(lax.broadcasted_iota(jnp.int32, (size, size), 0), ROWS) == lax.rem(
-        lax.broadcasted_iota(jnp.int32, (size, size), 1), ROWS
-    )
-    spread_low = spread[...]
 
     def wide_map(dims):
-        tall = dot(spread_low, skip[...], dims).astype(low)
-        full = dot(tall, spread_low, ((1,), (1,)))
+        same_row = lax.rem(lax.broadcasted_iota(jnp.int32, (size, size), 0), ROWS) == lax.rem(
+            lax.broadcasted_iota(jnp.int32, (size, size), 1), ROWS
+        )
+        tall = dot(spread[...], skip[...], dims).astype(low)
+        full = dot(tall, spread[...], ((1,), (1,)))
         return jnp.where(same_row, full, 0.0).astype(low)
 
-    skip_part[...] = dot(wide_map(((1,), (0,))), dens[...]) + bias[...]
-    back_map = wide_map(((1,), (1,)))
-
+    trans[...] = trans_back[...].astype(wide).T.astype(low)
+    forward_map = wide_map(((1,), (0,)))
     swap.wait_recv()
     mine = weight[...].astype(low).astype(wide)
     other = wrecv[...].astype(wide)[:, :channels]
@@ -329,54 +369,64 @@
     scale = keep * jnp.where(me == 0, 1.0, 2.0)
 
     def by_device(values):
-        return values.reshape(n, values.shape[0] // n, values.shape[1])
+        return values.reshape(n, values.shape[0] // n, values.shape[1]).astype(low)
 
     def flat(ref, stream):
         values = ref[stream]
         return values.reshape(values.shape[0] * values.shape[1], values.shape[2])
 
-    for stream in range(STREAMS):
-        wait_all(0, stream, a1r, a1r)
+    def flat_modes(ref, stream):
+        values = ref[stream].astype(wide)
+        return values.reshape(values.shape[0] * values.shape[1], values.shape[2]).astype(low)
+
+    for stream in range(STREAMS):
+        all_of(0, stream, a1r).wait_recv()
         a2s[stream] = by_device(dot(trans[...], flat(a1r, stream)))
         send_all(1, stream, a2s, a2r)
-    for stream in range(STREAMS):
-        wait_all(1, stream, a2s, a2r)
-        spectrum = dot(order[...], flat(a2r, stream).astype(low)).astype(low)
+    bias_column = jnp.sum(spread[...].astype(wide) * bias[...], axis=1, keepdims=True)
+    skip_part[...] = dot(forward_map, dens[...]) + bias_column
+    for stream in range(STREAMS):
+        all_of(1, stream, a2r).wait_recv()
+        spectrum = dot(order[...], flat_modes(a2r, stream)).astype(low)
         kept[stream] = spectrum
         mixed = (dot(mixer_back, spectrum) * scale).astype(low)
         b1s[stream] = by_device(dot(order_back[...], mixed))
         send_all(2, stream, b1s, b1r)
-    for stream in range(STREAMS):
-        wait_all(2, stream, b1s, b1r)
-        b2s[stream] = by_device(dot(trans_back[...], flat(b1r, stream).astype(low)).astype(low))
-        send_all(3, stream, b2s, b2r)
-    for stream in range(STREAMS):
-
-        def slope_block(device):
-            before = b2r[stream, device].astype(wide) + skip_part[rows(device), lanes(stream)]
+    back_map = wide_map(((1,), (1,)))
+    for stream in range(STREAMS):
+        all_of(2, stream, b1r).wait_recv()
+        b2s[stream] = by_device(dot(trans_back[...], flat_modes(b1r, stream)))
+        send_blocks(3, stream, b2s, b2r)
+    for stream in range(STREAMS):
+
+        def slope_block(device, cells):
+            before = cells.astype(wide) + skip_part[rows(device), lanes(stream)]
             cotangent = upst[rows(device), lanes(stream)].astype(wide)
             c1s[stream, device] = (cotangent * gelu_slope(before)).astype(low)
 
-        slope_block(me)
+        slope_block(me, b2s[stream, me])
         c1r[stream, me] = c1s[stream, me]
 
         def one_slope(step, carry):
             shift = n - step
             device = lax.rem(me + step, n)
-            remote(3, stream, shift, b2s.at[stream, me], b2r.at[stream, me]).wait_recv()
-            slope_block(device)
+            cells = b2r.at[stream, device]
+            remote(3, stream, step, cells, cells, block_sem.at[0, stream, shift]).wait_recv()
+            slope_block(device, cells[...])
             remote(4, stream, step, c1s.at[stream, device], c1r.at[stream, me]).start()
             return carry
 
         lax.fori_loop(1, n, one_slope, 0)
     for stream in range(STREAMS):
-        wait_all(4, stream, c1s, c1r)
+        all_of(4, stream, c1r).wait_recv()
         c2s[stream] = by_device(dot(trans[...], flat(c1r, stream)))
         send_all(5, stream, c2s, c2r)
+    for stream in range(STREAMS):
+        skip_part[:, lanes(stream)] = dot(back_map, flat(c1s, stream))
     products = jnp.zeros((2 * channels, 2 * channels), wide)
     for stream in range(STREAMS):
-        wait_all(5, stream, c2s, c2r)
-        gradient = (dot(order[...], flat(c2r, stream).astype(low)) * scale).astype(low)
+        all_of(5, stream, c2r).wait_recv()
+        gradient = (dot(order[...], flat_modes(c2r, stream)) * scale).astype(low)
         returned = dot(mixer, gradient).astype(low)
         d1s[stream] = by_device(dot(order_back[...], returned))
         send_all(6, stream, d1s, d1r)
@@ -397,51 +447,34 @@
     )
     swap_grad.start()
     for stream in range(STREAMS):
-        wait_all(6, stream, d1s, d1r)
-        d2s[stream] = by_device(dot(trans_back[...], flat(d1r, stream).astype(low)).astype(low))
-        send_all(7, stream, d2s, d2r)
-    for stream in range(STREAMS):
-        skip_part[:, lanes(stream)] = dot(back_map, flat(c1s, stream))
+        all_of(6, stream, d1r).wait_recv()
+        d2s[stream] = by_device(dot(trans_back[...], flat_modes(d1r, stream)))
+        send_blocks(7, stream, d2s, d2r)
     swap_grad.wait_recv()
-    weight_grad = ours + grecv[...][:, :channels]
-    one = beta_first * first[...] + (1.0 - beta_first) * weight_grad
-    two = beta_second * second[...] + (1.0 - beta_second) * weight_grad * weight_grad
-    new_first[...] = one
-    new_second[...] = two
-    first_hat = one / (1.0 - beta_first**STEP)
-    second_hat = two / (1.0 - beta_second**STEP)
-    new_weight[...] = weight[...] - learn_rate * (
-        first_hat / (jnp.sqrt(second_hat) + epsilon) + decay_rate * weight[...]
-    )
-    for stream in range(STREAMS):
-
-        def final_block(device):
-            total = d2r[stream, device].astype(wide) + skip_part[rows(device), lanes(stream)]
+    out_grad[...] = ours + grecv[...][:, :channels]
+    swap.wait_send()
+    swap_grad.wait_send()
+    for stage, source in enumerate((a1r, a2r, b1r, b2r, c1r, c2r, d1r)):
+        for stream in range(STREAMS):
+            all_of(stage, stream, source).wait_send()
+    for stream in range(STREAMS):
+
+        def final_block(device, cells):
+            total = cells.astype(wide) + skip_part[rows(device), lanes(stream)]
             out[rows(device), lanes(stream)] = total.astype(low)
 
-        final_block(me)
+        final_block(me, d2s[stream, me])
 
         def one_final(step, carry):
             shift = n - step
-            remote(7, stream, shift, d2s.at[stream, me], d2r.at[stream, me]).wait_recv()
-            final_block(lax.rem(me + step, n))
+            device = lax.rem(me + step, n)
+            cells = d2r.at[stream, device]
+            remote(7, stream, step, cells, cells, block_sem.at[1, stream, shift]).wait_recv()
+            final_block(device, cells[...])
             return carry
 
         lax.fori_loop(1, n, one_final, 0)
-
-    swap.wait_send()
-    swap_grad.wait_send()
-    sources = (a1r, a2s, b1s, b2s, c1s, c2s, d1s, d2s)
-    for stage, source in enumerate(sources):
-        for stream in range(STREAMS):
-
-            def sent(shift, carry):
-                remote(
-                    stage, stream, shift, source.at[stream, me], source.at[stream, me]
-                ).wait_send()
-                return carry
-
-            lax.fori_loop(1, n, sent, 0)
+        all_of(7, stream, d2r).wait_send()
 
 
 def one_frequency_each(
@@ -454,63 +487,62 @@
     tables = fixed_tables(n, own, slab_rows)
     low, wide = jnp.bfloat16, jnp.float32
     vmem = pl.BlockSpec(memory_space=pltpu.VMEM)
+    hbm = pl.BlockSpec(memory_space=pltpu.HBM)
     cells = pltpu.VMEM((STREAMS, n, own * slab_rows, width), low)
-    modes = pltpu.VMEM((STREAMS, n, 2 * own, width), wide)
-    result = pl.pallas_call(
+    modes = pltpu.VMEM((STREAMS, n, 2 * own, width), low)
+    arrays = (
+        density.reshape(size, line_count),
+        upstream.reshape(size, line_count),
+        spectral_weight,
+        skip_weight,
+        skip_bias.reshape(1, channels),
+    )
+    input_grad, weight_grad = pl.pallas_call(
         functools.partial(step_kernel, n),
         out_shape=(
             jax.ShapeDtypeStruct((size, line_count), low),
             jax.ShapeDtypeStruct((channels, channels), wide),
-            jax.ShapeDtypeStruct((channels, channels), wide),
-            jax.ShapeDtypeStruct((channels, channels), wide),
         ),
-        in_specs=[vmem] * 7 + [pl.BlockSpec(memory_space=pltpu.SMEM)] + [vmem] * 5,
-        out_specs=(vmem,) * 4,
-        scratch_shapes=[
-            cells,
-            modes,
-            modes,
-            modes,
-            modes,
-            cells,
-            cells,
-            cells,
-            cells,
-            modes,
-            modes,
-            modes,
-            modes,
-            cells,
-            cells,
+        in_specs=[hbm] * 5 + [pl.BlockSpec(memory_space=pltpu.SMEM)] + [hbm] * 4,
+        out_specs=(vmem,) * 2,
+        scratch_shapes=[pltpu.VMEM(each.shape, each.dtype) for each in arrays + tables]
+        + [pltpu.VMEM(tables[0].shape[::-1], low)]
+        + [cells, modes, modes, modes, modes, cells, cells]
+        + [cells, cells, modes, modes, modes, modes, cells, cells]
+        + [
             pltpu.VMEM((size, line_count), wide),
             pltpu.VMEM((STREAMS, 2 * channels, width), low),
             pltpu.VMEM((channels, 2 * channels), low),
             pltpu.VMEM((channels, 2 * channels), low),
             pltpu.VMEM((channels, 2 * channels), wide),
             pltpu.VMEM((channels, 2 * channels), wide),
-            pltpu.SemaphoreType.DMA((8, STREAMS, n)),
-            pltpu.SemaphoreType.DMA((8, STREAMS, n)),
+            pltpu.SemaphoreType.DMA((8, STREAMS)),
+            pltpu.SemaphoreType.DMA((8, STREAMS)),
+            pltpu.SemaphoreType.DMA((2, STREAMS, n)),
             pltpu.SemaphoreType.DMA((2,)),
             pltpu.SemaphoreType.DMA((2,)),
+            pltpu.SemaphoreType.DMA((9,)),
         ],
         compiler_params=pltpu.CompilerParams(
-            collective_id=0, has_side_effects=True, vmem_limit_bytes=40 * 1024 * 1024
+            collective_id=0, has_side_effects=True, vmem_limit_bytes=60 * 1024 * 1024
         ),
         cost_estimate=pl.CostEstimate(
             flops=1_000_000_000, bytes_accessed=2_000_000, transcendentals=300_000
         ),
-    )(
-        density.reshape(size, line_count),
-        upstream.reshape(size, line_count),
-        spectral_weight,
-        moment_one,
-        moment_two,
-        skip_weight,
-        jnp.repeat(skip_bias, slab_rows)[:, None],
-        mode_counts,
-        *tables,
-    )
-    return (result[0].reshape(density.shape), *result[1:])
+    )(*arrays, mode_counts, *tables)
+    updated = adam(weight_grad, spectral_weight, moment_one, moment_two)
+    return (input_grad.reshape(density.shape), *updated)
+
+
+def adam(weight_grad, spectral_weight, moment_one, moment_two):
+    new_moment_one = beta_first * moment_one + (1.0 - beta_first) * weight_grad
+    new_moment_two = beta_second * moment_two + (1.0 - beta_second) * weight_grad * weight_grad
+    first_hat = new_moment_one / (1.0 - beta_first**STEP)
+    second_hat = new_moment_two / (1.0 - beta_second**STEP)
+    new_weight = spectral_weight - learn_rate * (
+        first_hat / (jnp.sqrt(second_hat) + epsilon) + decay_rate * spectral_weight
+    )
+    return (new_weight, new_moment_one, new_moment_two)
 
 
 def on_mesh(density, *others):

time: 71.3 us -> 56.8 us (0.80)
  local copies, waits for them, and re-layouts: 10.8 us -> 1.68 us
  Pallas kernels: 59.4 us -> 52.7 us
  other arithmetic: 0 us -> 1.41 us
    unnamed x28 -> x7, local copies, waits for them, and re-layouts: 9.86 us -> 1.68 us
    pallas_call x1, Pallas kernels: 59.4 us -> 52.7 us  [one_frequency_each(): pl.pallas_call(functools.partial(step_kernel, n), out_shape=(jax.ShapeDty...]
    sub x0 -> x1, other arithmetic: none -> 1.41 us  [adam(): spectral_weight - learn_rate * (first_hat / (jnp.sqrt(second_hat) + epsil...]
    broadcast_in_dim x1 -> x0, local copies, waits for them, and re-layouts: 0.77 us -> none  [one_frequency_each(): jnp.repeat(skip_bias, slab_rows)[:, None]]
where the time goes in v2:
time: 56.8 us; the launch traced here: 56.5 us
  Pallas kernels  52.7 us (93%)
  local copies, waits for them, and re-layouts  1.68 us (3%)
  other arithmetic  1.41 us (2%)
  between operations  0.69 us (1%)
    pallas_call x1, Pallas kernels, one_frequency_each(): pl.pallas_call(functools.partial(step_kernel, n), out_shape=(jax.ShapeDty...  52.7 us
    unnamed x7, local copies, waits for them, and re-layouts  1.68 us
    sub x1, other arithmetic, adam(): spectral_weight - learn_rate * (first_hat / (jnp.sqrt(second_hat) + epsil...  1.41 us

profile of v2, /device:TPU:0, one launch (start us, length us, event | category | flops | bytes accessed | tf_op | source)
XLA Modules:
  0.0 56.5 jit_solution(17540473912165963420)
XLA Ops:
  0.6 0.0 copy-start
  0.6 0.0 copy-start.1
  0.7 0.0 copy-start.2
  0.7 52.7 %shard_map.147 = (bf16[512,256]{1,0:T(8,128)(2,1)}, f32[64,64]{1,0:T(8,128)}) custom-call(bf16[512,256]{1,0:T(8,128)(2,1)} %bitcast.5, bf16[512,256]{1,0:T(8,128)(2,1)} %bitcast.6, f32[64,64]{1,0:T(8,128)} %weight_hbm.1, bf16[64,64]{1,0:T(8,128)(2,1)} %skip_hbm.1, f32[1,64]{1,0:T(1,128)} %bitcast.7, s32[2]{0:T(128)} %counts.1, ...), custom_call_target="tpu_custom_call" | custom-call | flops 1000000000 | bytes 2000000 | tf_op jit(solution)/shard_map/pallas_call | solution.py:500
  53.4 0.0 copy-done
  53.4 0.0 copy-done.1
  53.4 0.0 copy-done.2
  53.4 1.4 %multiply_subtract_fusion = (f32[64,64]{1,0:T(8,128)}, f32[64,64]{1,0:T(8,128)}, f32[64,64]{1,0:T(8,128)}) fusion(f32[64,64]{1,0:T(8,128)S(1)} %copy-done, f32[64,64]{1,0:T(8,128)} %get-tuple-element.7, f32[64,64]{1,0:T(8,128)S(1)} %copy-done.1, f32[64,64]{1,0:T(8,128)S(1)} %copy-done.2), kind=kLoop, calls=%fused_computation.2 | loop fusion | flops 61440 | bytes 114688 | tf_op jit(solution)/shard_map/sub | solution.py:542
  54.8 1.7 %copy.17 = bf16[1,64,8,256]{3,2,1,0:T(8,128)(2,1)} copy(bf16[1,64,8,256]{3,2,1,0:T(8,128)(2,1)} %bitcast.4) | data formatting | bytes 524288
Async XLA Ops:
  0.6 52.8 %copy-start = (f32[64,64]{1,0:T(8,128)S(1)}, f32[64,64]{1,0:T(8,128)}, u32[]{:S(2)}) copy-start(f32[64,64]{1,0:T(8,128)} %weight_hbm.1) | copy-start | bytes 49156
  0.6 52.8 %copy-start.1 = (f32[64,64]{1,0:T(8,128)S(1)}, f32[64,64]{1,0:T(8,128)}, u32[]{:S(2)}) copy-start(f32[64,64]{1,0:T(8,128)} %param.15) | copy-start | bytes 49156
  0.7 52.8 %copy-start.2 = (f32[64,64]{1,0:T(8,128)S(1)}, f32[64,64]{1,0:T(8,128)}, u32[]{:S(2)}) copy-start(f32[64,64]{1,0:T(8,128)} %param.16) | copy-start | bytes 49156

commit v3 on v2

--- a/solution.py
+++ b/solution.py
@@ -263,8 +263,12 @@
         return carry
 
     lax.fori_loop(1, n, greet, 0, unroll=True)
-    pl.semaphore_signal(barrier, inc=1, device_id=(1 - core, me), device_id_type=MESH)
-    pl.semaphore_wait(barrier, n)
+    pl.semaphore_wait(barrier, n - 1 + core)
+
+    @pl.when(core == 0)
+    def _():
+        pl.semaphore_signal(barrier, inc=1, device_id=(1 - core, me), device_id_type=MESH)
+
     loads[0].wait()
 
     def remote(stage, stream, shift, source, target, arrival=None):
@@ -334,7 +338,11 @@
         device_id=(1 - core, me),
         device_id_type=MESH,
     )
-    swap.start()
+
+    @pl.when(core == 1)
+    def _():
+        swap.start()
+
     for load in loads[2:]:
         load.wait()
 
@@ -350,7 +358,29 @@
 
     trans[...] = trans_back[...].astype(wide).T.astype(low)
     forward_map = wide_map(((1,), (0,)))
+    def by_device(values):
+        return values.reshape(n, values.shape[0] // n, values.shape[1]).astype(low)
+
+    def flat(ref, stream):
+        values = ref[stream]
+        return values.reshape(values.shape[0] * values.shape[1], values.shape[2])
+
+    def flat_modes(ref, stream):
+        values = ref[stream].astype(wide)
+        return values.reshape(values.shape[0] * values.shape[1], values.shape[2]).astype(low)
+
+    for stream in range(STREAMS):
+        all_of(0, stream, a1r).wait_recv()
+        a2s[stream] = by_device(dot(trans[...], flat(a1r, stream)))
+        send_all(1, stream, a2s, a2r)
+    bias_column = jnp.sum(spread[...].astype(wide) * bias[...], axis=1, keepdims=True)
+    skip_part[...] = dot(forward_map, dens[...]) + bias_column
     swap.wait_recv()
+
+    @pl.when(core == 0)
+    def _():
+        swap.start()
+
     mine = weight[...].astype(low).astype(wide)
     other = wrecv[...].astype(wide)[:, :channels]
     is_first = core == 0
@@ -368,23 +398,6 @@
     keep = jnp.where(me < counts[core], 1.0, 0.0)
     scale = keep * jnp.where(me == 0, 1.0, 2.0)
 
-    def by_device(values):
-        return values.reshape(n, values.shape[0] // n, values.shape[1]).astype(low)
-
-    def flat(ref, stream):
-        values = ref[stream]
-        return values.reshape(values.shape[0] * values.shape[1], values.shape[2])
-
-    def flat_modes(ref, stream):
-        values = ref[stream].astype(wide)
-        return values.reshape(values.shape[0] * values.shape[1], values.shape[2]).astype(low)
-
-    for stream in range(STREAMS):
-        all_of(0, stream, a1r).wait_recv()
-        a2s[stream] = by_device(dot(trans[...], flat(a1r, stream)))
-        send_all(1, stream, a2s, a2r)
-    bias_column = jnp.sum(spread[...].astype(wide) * bias[...], axis=1, keepdims=True)
-    skip_part[...] = dot(forward_map, dens[...]) + bias_column
     for stream in range(STREAMS):
         all_of(1, stream, a2r).wait_recv()
         spectrum = dot(order[...], flat_modes(a2r, stream)).astype(low)

time: 56.8 us -> 58.4 us (1.028)
  Pallas kernels: 52.7 us -> 54.3 us
    pallas_call x1, Pallas kernels: 52.7 us -> 54.3 us  [one_frequency_each(): pl.pallas_call(functools.partial(step_kernel, n), out_shape=(jax.ShapeDty...]
where the time goes in v3:
time: 58.4 us; the launch traced here: 58.1 us
  Pallas kernels  54.3 us (93%)
  local copies, waits for them, and re-layouts  1.68 us (3%)
  other arithmetic  1.41 us (2%)
  between operations  0.69 us (1%)
    pallas_call x1, Pallas kernels, one_frequency_each(): pl.pallas_call(functools.partial(step_kernel, n), out_shape=(jax.ShapeDty...  54.3 us
    unnamed x7, local copies, waits for them, and re-layouts  1.68 us
    sub x1, other arithmetic, adam(): spectral_weight - learn_rate * (first_hat / (jnp.sqrt(second_hat) + epsil...  1.41 us

profile of v3, /device:TPU:0, one launch (start us, length us, event | category | flops | bytes accessed | tf_op | source)
XLA Modules:
  0.0 58.1 jit_solution(16451947798041288314)
XLA Ops:
  0.6 0.0 copy-start
  0.6 0.0 copy-start.1
  0.7 0.0 copy-start.2
  0.7 54.3 %shard_map.147 = (bf16[512,256]{1,0:T(8,128)(2,1)}, f32[64,64]{1,0:T(8,128)}) custom-call(bf16[512,256]{1,0:T(8,128)(2,1)} %bitcast.5, bf16[512,256]{1,0:T(8,128)(2,1)} %bitcast.6, f32[64,64]{1,0:T(8,128)} %weight_hbm.1, bf16[64,64]{1,0:T(8,128)(2,1)} %skip_hbm.1, f32[1,64]{1,0:T(1,128)} %bitcast.7, s32[2]{0:T(128)} %counts.1, ...), custom_call_target="tpu_custom_call" | custom-call | flops 1000000000 | bytes 2000000 | tf_op jit(solution)/shard_map/pallas_call | solution.py:513
  55.0 0.0 copy-done
  55.0 0.0 copy-done.1
  55.0 0.0 copy-done.2
  55.0 1.4 %multiply_subtract_fusion = (f32[64,64]{1,0:T(8,128)}, f32[64,64]{1,0:T(8,128)}, f32[64,64]{1,0:T(8,128)}) fusion(f32[64,64]{1,0:T(8,128)S(1)} %copy-done, f32[64,64]{1,0:T(8,128)} %get-tuple-element.7, f32[64,64]{1,0:T(8,128)S(1)} %copy-done.1, f32[64,64]{1,0:T(8,128)S(1)} %copy-done.2), kind=kLoop, calls=%fused_computation.2 | loop fusion | flops 61440 | bytes 114688 | tf_op jit(solution)/shard_map/sub | solution.py:555
  56.4 1.7 %copy.17 = bf16[1,64,8,256]{3,2,1,0:T(8,128)(2,1)} copy(bf16[1,64,8,256]{3,2,1,0:T(8,128)(2,1)} %bitcast.4) | data formatting | bytes 524288
Async XLA Ops:
  0.6 54.4 %copy-start = (f32[64,64]{1,0:T(8,128)S(1)}, f32[64,64]{1,0:T(8,128)}, u32[]{:S(2)}) copy-start(f32[64,64]{1,0:T(8,128)} %weight_hbm.1) | copy-start | bytes 49156
  0.6 54.4 %copy-start.1 = (f32[64,64]{1,0:T(8,128)S(1)}, f32[64,64]{1,0:T(8,128)}, u32[]{:S(2)}) copy-start(f32[64,64]{1,0:T(8,128)} %param.15) | copy-start | bytes 49156
  0.7 54.4 %copy-start.2 = (f32[64,64]{1,0:T(8,128)S(1)}, f32[64,64]{1,0:T(8,128)}, u32[]{:S(2)}) copy-start(f32[64,64]{1,0:T(8,128)} %param.16) | copy-start | bytes 49156

commit v4 on v2

--- a/solution.py
+++ b/solution.py
@@ -148,7 +148,7 @@
 
 MESH = pl.DeviceIdType.MESH
 ROWS = 8
-STREAMS = 2
+STREAMS = 1
 
 
 def fixed_tables(devices, own, rows):

time: 56.8 us -> 59.8 us (1.053)
  Pallas kernels: 52.7 us -> 55.8 us
    pallas_call x1, Pallas kernels: 52.7 us -> 55.8 us  [one_frequency_each(): pl.pallas_call(functools.partial(step_kernel, n), out_shape=(jax.ShapeDty...]
where the time goes in v4:
time: 59.8 us; the launch traced here: 59.5 us
  Pallas kernels  55.8 us (93%)
  local copies, waits for them, and re-layouts  1.68 us (3%)
  other arithmetic  1.41 us (2%)
  between operations  0.69 us (1%)
    pallas_call x1, Pallas kernels, one_frequency_each(): pl.pallas_call(functools.partial(step_kernel, n), out_shape=(jax.ShapeDty...  55.8 us
    unnamed x7, local copies, waits for them, and re-layouts  1.68 us
    sub x1, other arithmetic, adam(): spectral_weight - learn_rate * (first_hat / (jnp.sqrt(second_hat) + epsil...  1.41 us

profile of v4, /device:TPU:0, one launch (start us, length us, event | category | flops | bytes accessed | tf_op | source)
XLA Modules:
  0.0 59.5 jit_solution(14248695796229631448)
XLA Ops:
  0.6 0.0 copy-start
  0.6 0.0 copy-start.1
  0.7 0.0 copy-start.2
  0.7 55.8 %shard_map.147 = (bf16[512,256]{1,0:T(8,128)(2,1)}, f32[64,64]{1,0:T(8,128)}) custom-call(bf16[512,256]{1,0:T(8,128)(2,1)} %bitcast.5, bf16[512,256]{1,0:T(8,128)(2,1)} %bitcast.6, f32[64,64]{1,0:T(8,128)} %weight_hbm.1, bf16[64,64]{1,0:T(8,128)(2,1)} %skip_hbm.1, f32[1,64]{1,0:T(1,128)} %bitcast.7, s32[2]{0:T(128)} %counts.1, ...), custom_call_target="tpu_custom_call" | custom-call | flops 1000000000 | bytes 2000000 | tf_op jit(solution)/shard_map/pallas_call | solution.py:500
  56.4 0.0 copy-done
  56.4 0.0 copy-done.1
  56.5 0.0 copy-done.2
  56.5 1.4 %multiply_subtract_fusion = (f32[64,64]{1,0:T(8,128)}, f32[64,64]{1,0:T(8,128)}, f32[64,64]{1,0:T(8,128)}) fusion(f32[64,64]{1,0:T(8,128)S(1)} %copy-done, f32[64,64]{1,0:T(8,128)} %get-tuple-element.7, f32[64,64]{1,0:T(8,128)S(1)} %copy-done.1, f32[64,64]{1,0:T(8,128)S(1)} %copy-done.2), kind=kLoop, calls=%fused_computation.2 | loop fusion | flops 61440 | bytes 114688 | tf_op jit(solution)/shard_map/sub | solution.py:542
  57.9 1.7 %copy.17 = bf16[1,64,8,256]{3,2,1,0:T(8,128)(2,1)} copy(bf16[1,64,8,256]{3,2,1,0:T(8,128)(2,1)} %bitcast.4) | data formatting | bytes 524288
Async XLA Ops:
  0.6 55.8 %copy-start = (f32[64,64]{1,0:T(8,128)S(1)}, f32[64,64]{1,0:T(8,128)}, u32[]{:S(2)}) copy-start(f32[64,64]{1,0:T(8,128)} %weight_hbm.1) | copy-start | bytes 49156
  0.6 55.8 %copy-start.1 = (f32[64,64]{1,0:T(8,128)S(1)}, f32[64,64]{1,0:T(8,128)}, u32[]{:S(2)}) copy-start(f32[64,64]{1,0:T(8,128)} %param.15) | copy-start | bytes 49156
  0.7 55.8 %copy-start.2 = (f32[64,64]{1,0:T(8,128)S(1)}, f32[64,64]{1,0:T(8,128)}, u32[]{:S(2)}) copy-start(f32[64,64]{1,0:T(8,128)} %param.16) | copy-start | bytes 49156

commit v5 on v2

--- a/solution.py
+++ b/solution.py
@@ -149,31 +149,41 @@
 MESH = pl.DeviceIdType.MESH
 ROWS = 8
 STREAMS = 2
-
-
-def fixed_tables(devices, own, rows):
-    cells = devices * rows
+HALVES = 2
+LANES = 128
+
+
+def fixed_tables(halves, members, own, rows):
+    cells = halves * members * rows
     freq = np.arange(MODES)[:, None]
     angles = 2.0 * np.pi * ((freq * np.arange(cells)[None, :]) % cells) / cells
     scaling = 1.0 / math.sqrt(cells)
     parts = np.stack([np.cos(angles) * scaling, -np.sin(angles) * scaling], 1)
-    parts = parts.reshape(MODES, 2, 1, devices, 1, rows)
-    same = np.eye(own).reshape(1, 1, own, 1, own, 1)
-    transform = (parts * same).reshape(MODES * 2 * own, devices * own * rows)
-    channels = devices * own
-    order = np.zeros((2, devices, own, devices, 2, own))
+    parts = parts.reshape(MODES, 2, halves, members, rows).transpose(2, 3, 4, 0, 1)
+    parts = parts.reshape(halves, members, 1, rows, MODES, 2, 1)
+    same = np.eye(own).reshape(1, 1, own, 1, 1, 1, own)
+    transform = (parts * same).reshape(halves, members * own * rows, -1, LANES)
+    transform = transform.transpose(0, 2, 1, 3)
+    channels = members * own
+    order = np.zeros((2, members, own, members, 2, own))
     for part in range(2):
-        for device in range(devices):
+        for device in range(members):
             for one in range(own):
                 order[part, device, one, device, part, one] = 1.0
     order = order.reshape(2 * channels, 2 * channels)
     spread = np.repeat(np.eye(channels), rows, axis=0)
     low = lambda table: jnp.asarray(table.astype(np.float32), jnp.bfloat16)
-    return low(transform.T), low(order), low(order.T), low(spread)
+    return low(transform), low(order), low(order.T), low(spread)
 
 
 def dot(left, right, dims=((1,), (0,))):
     return lax.dot_general(left, right, (dims, ((), ())), preferred_element_type=jnp.float32)
+
+
+def exact_dot(left, right):
+    return jnp.dot(
+        left, right, precision=lax.Precision.HIGHEST, preferred_element_type=jnp.float32
+    )
 
 
 def step_kernel(
@@ -231,7 +241,9 @@
     me = lax.axis_index("dom")
     core = lax.axis_index("dp")
     low, wide = jnp.bfloat16, jnp.float32
-    block = dens.shape[0] // n
+    members = n // HALVES
+    half, member = me // members, lax.rem(me, members)
+    block = dens.shape[0] // members
     width = dens.shape[1] // STREAMS
     channels = weight.shape[0]
 
@@ -246,7 +258,10 @@
                 (bias_hbm, bias),
                 (order_hbm, order),
                 (order_back_hbm, order_back),
-                (trans_back_hbm, trans_back),
+                *(
+                    (trans_back_hbm.at[half, tile], trans_back.at[:, pl.ds(tile * LANES, LANES)])
+                    for tile in range(trans_back_hbm.shape[1])
+                ),
                 (upst_hbm, upst),
             )
         )
@@ -267,43 +282,52 @@
     pl.semaphore_wait(barrier, n)
     loads[0].wait()
 
-    def remote(stage, stream, shift, source, target, arrival=None):
+    def remote(stage, stream, peer, source, target, arrival=None):
         return pltpu.make_async_remote_copy(
             src_ref=source,
             dst_ref=target,
             send_sem=send_sem.at[stage, stream],
             recv_sem=recv_sem.at[stage, stream] if arrival is None else arrival,
-            device_id=(core, lax.rem(me + shift, n)),
+            device_id=(core, peer),
             device_id_type=MESH,
         )
 
-    def send_all(stage, stream, source, target):
-        def one(shift, carry):
-            peer = lax.rem(me + shift, n)
-            remote(stage, stream, shift, source.at[stream, peer], target.at[stream, me]).start()
-            return carry
-
-        lax.fori_loop(1, n, one, 0, unroll=True)
-        target[stream, me] = source[stream, me]
-
-    def send_blocks(stage, stream, source, target):
+    def send_modes(stage, stream, source, target, slots):
         def one(shift, carry):
             peer = lax.rem(me + shift, n)
             remote(
                 stage,
                 stream,
-                shift,
+                peer,
+                source.at[stream, lax.rem(peer, slots)],
+                target.at[stream, me],
+            ).start()
+            return carry
+
+        lax.fori_loop(1, n, one, 0, unroll=True)
+        target[stream, me] = source[stream, lax.rem(me, slots)]
+
+    def near(step):
+        return lax.rem(member + step, members)
+
+    def send_blocks(stage, stream, source, target):
+        def one(shift, carry):
+            peer = near(shift)
+            remote(
+                stage,
+                stream,
+                half * members + peer,
                 source.at[stream, peer],
-                target.at[stream, me],
+                target.at[stream, member],
                 block_sem.at[stage // 4, stream, shift],
             ).start()
             return carry
 
-        lax.fori_loop(1, n, one, 0, unroll=True)
+        lax.fori_loop(1, members, one, 0, unroll=True)
 
     def all_of(stage, stream, ref):
-        blocks = ref.at[stream, pl.ds(0, n - 1)]
-        return remote(stage, stream, 1, blocks, blocks)
+        blocks = ref.at[stream, pl.ds(0, ref.shape[1] - 1)]
+        return remote(stage, stream, me, blocks, blocks)
 
     def lanes(stream):
         return pl.ds(stream * width, width)
@@ -314,14 +338,18 @@
     for stream in range(STREAMS):
 
         def start_one(shift, carry):
-            peer = lax.rem(me + shift, n)
+            peer = near(shift)
             remote(
-                0, stream, shift, dens.at[rows(peer), lanes(stream)], a1r.at[stream, me]
+                0,
+                stream,
+                half * members + peer,
+                dens.at[rows(peer), lanes(stream)],
+                a1r.at[stream, member],
             ).start()
             return carry
 
-        lax.fori_loop(1, n, start_one, 0, unroll=True)
-        a1r[stream, me] = dens[rows(me), lanes(stream)]
+        lax.fori_loop(1, members, start_one, 0, unroll=True)
+        a1r[stream, member] = dens[rows(member), lanes(stream)]
 
     loads[1].wait()
     own_low = weight[...].astype(low)
@@ -363,39 +391,42 @@
         ],
         axis=0,
     )
+    mixer = dot(dot(order_back[...], mixer.astype(low)).astype(low), order[...])
     mixer_back = mixer.T.astype(low)
     mixer = mixer.astype(low)
     keep = jnp.where(me < counts[core], 1.0, 0.0)
     scale = keep * jnp.where(me == 0, 1.0, 2.0)
 
-    def by_device(values):
-        return values.reshape(n, values.shape[0] // n, values.shape[1]).astype(low)
+    def blocks_of(values, count):
+        return values.astype(low).reshape(count, values.shape[0] // count, values.shape[1])
 
     def flat(ref, stream):
         values = ref[stream]
         return values.reshape(values.shape[0] * values.shape[1], values.shape[2])
 
-    def flat_modes(ref, stream):
+    def added(ref, stream):
         values = ref[stream].astype(wide)
-        return values.reshape(values.shape[0] * values.shape[1], values.shape[2]).astype(low)
+        total = values[:members]
+        for other in range(1, HALVES):
+            total += values[other * members : (other + 1) * members]
+        return total.reshape(members * values.shape[1], values.shape[2])
 
     for stream in range(STREAMS):
         all_of(0, stream, a1r).wait_recv()
-        a2s[stream] = by_device(dot(trans[...], flat(a1r, stream)))
-        send_all(1, stream, a2s, a2r)
+        a2s[stream] = blocks_of(dot(trans[...], flat(a1r, stream)), n)
+        send_modes(1, stream, a2s, a2r, n)
     bias_column = jnp.sum(spread[...].astype(wide) * bias[...], axis=1, keepdims=True)
     skip_part[...] = dot(forward_map, dens[...]) + bias_column
     for stream in range(STREAMS):
         all_of(1, stream, a2r).wait_recv()
-        spectrum = dot(order[...], flat_modes(a2r, stream)).astype(low)
+        spectrum = added(a2r, stream).astype(low)
         kept[stream] = spectrum
-        mixed = (dot(mixer_back, spectrum) * scale).astype(low)
-        b1s[stream] = by_device(dot(order_back[...], mixed))
-        send_all(2, stream, b1s, b1r)
+        b1s[stream] = blocks_of(dot(mixer_back, spectrum) * scale, members)
+        send_modes(2, stream, b1s, b1r, members)
     back_map = wide_map(((1,), (1,)))
     for stream in range(STREAMS):
         all_of(2, stream, b1r).wait_recv()
-        b2s[stream] = by_device(dot(trans_back[...], flat_modes(b1r, stream)))
+        b2s[stream] = blocks_of(dot(trans_back[...], flat(b1r, stream)), members)
         send_blocks(3, stream, b2s, b2r)
     for stream in range(STREAMS):
 
@@ -404,33 +435,40 @@
             cotangent = upst[rows(device), lanes(stream)].astype(wide)
             c1s[stream, device] = (cotangent * gelu_slope(before)).astype(low)
 
-        slope_block(me, b2s[stream, me])
-        c1r[stream, me] = c1s[stream, me]
+        slope_block(member, b2s[stream, member])
+        c1r[stream, member] = c1s[stream, member]
 
         def one_slope(step, carry):
-            shift = n - step
-            device = lax.rem(me + step, n)
+            device = near(step)
             cells = b2r.at[stream, device]
-            remote(3, stream, step, cells, cells, block_sem.at[0, stream, shift]).wait_recv()
+            remote(
+                3, stream, me, cells, cells, block_sem.at[0, stream, members - step]
+            ).wait_recv()
             slope_block(device, cells[...])
-            remote(4, stream, step, c1s.at[stream, device], c1r.at[stream, me]).start()
+            remote(
+                4,
+                stream,
+                half * members + device,
+                c1s.at[stream, device],
+                c1r.at[stream, member],
+            ).start()
             return carry
 
-        lax.fori_loop(1, n, one_slope, 0)
+        lax.fori_loop(1, members, one_slope, 0)
     for stream in range(STREAMS):
         all_of(4, stream, c1r).wait_recv()
-        c2s[stream] = by_device(dot(trans[...], flat(c1r, stream)))
-        send_all(5, stream, c2s, c2r)
+        c2s[stream] = blocks_of(dot(trans[...], flat(c1r, stream)), n)
+        send_modes(5, stream, c2s, c2r, n)
     for stream in range(STREAMS):
         skip_part[:, lanes(stream)] = dot(back_map, flat(c1s, stream))
     products = jnp.zeros((2 * channels, 2 * channels), wide)
     for stream in range(STREAMS):
         all_of(5, stream, c2r).wait_recv()
-        gradient = (dot(order[...], flat_modes(c2r, stream)) * scale).astype(low)
-        returned = dot(mixer, gradient).astype(low)
-        d1s[stream] = by_device(dot(order_back[...], returned))
-        send_all(6, stream, d1s, d1r)
+        gradient = (added(c2r, stream) * scale).astype(low)
+        d1s[stream] = blocks_of(dot(mixer, gradient), members)
+        send_modes(6, stream, d1s, d1r, members)
         products += dot(kept[stream], gradient, ((1,), (1,)))
+    products = exact_dot(exact_dot(order[...].astype(wide), products), order_back[...].astype(wide))
     top, bottom = products[:channels], products[channels:]
     grad_real = top[:, :channels] + bottom[:, channels:]
     grad_imag = top[:, channels:] - bottom[:, :channels]
@@ -448,7 +486,7 @@
     swap_grad.start()
     for stream in range(STREAMS):
         all_of(6, stream, d1r).wait_recv()
-        d2s[stream] = by_device(dot(trans_back[...], flat_modes(d1r, stream)))
+        d2s[stream] = blocks_of(dot(trans_back[...], flat(d1r, stream)), members)
         send_blocks(7, stream, d2s, d2r)
     swap_grad.wait_recv()
     out_grad[...] = ours + grecv[...][:, :channels]
@@ -463,17 +501,18 @@
             total = cells.astype(wide) + skip_part[rows(device), lanes(stream)]
             out[rows(device), lanes(stream)] = total.astype(low)
 
-        final_block(me, d2s[stream, me])
+        final_block(member, d2s[stream, member])
 
         def one_final(step, carry):
-            shift = n - step
-            device = lax.rem(me + step, n)
+            device = near(step)
             cells = d2r.at[stream, device]
-            remote(7, stream, step, cells, cells, block_sem.at[1, stream, shift]).wait_recv()
+            remote(
+                7, stream, me, cells, cells, block_sem.at[1, stream, members - step]
+            ).wait_recv()
             final_block(device, cells[...])
             return carry
 
-        lax.fori_loop(1, n, one_final, 0)
+        lax.fori_loop(1, members, one_final, 0)
         all_of(7, stream, d2r).wait_send()
 
 
@@ -481,15 +520,17 @@
     n, density, upstream, spectral_weight, moment_one, moment_two, skip_weight, skip_bias, mode_counts
 ):
     samples, channels, slab_rows, line_count = density.shape
-    own = channels // n
+    members = n // HALVES
+    own = channels // members
     width = line_count // STREAMS
     size = channels * slab_rows
-    tables = fixed_tables(n, own, slab_rows)
+    tables = fixed_tables(HALVES, members, own, slab_rows)
     low, wide = jnp.bfloat16, jnp.float32
     vmem = pl.BlockSpec(memory_space=pltpu.VMEM)
     hbm = pl.BlockSpec(memory_space=pltpu.HBM)
-    cells = pltpu.VMEM((STREAMS, n, own * slab_rows, width), low)
+    cells = pltpu.VMEM((STREAMS, members, own * slab_rows, width), low)
     modes = pltpu.VMEM((STREAMS, n, 2 * own, width), low)
+    mixed = pltpu.VMEM((STREAMS, members, 2 * own, width), low)
     arrays = (
         density.reshape(size, line_count),
         upstream.reshape(size, line_count),
@@ -505,10 +546,12 @@
         ),
         in_specs=[hbm] * 5 + [pl.BlockSpec(memory_space=pltpu.SMEM)] + [hbm] * 4,
         out_specs=(vmem,) * 2,
-        scratch_shapes=[pltpu.VMEM(each.shape, each.dtype) for each in arrays + tables]
-        + [pltpu.VMEM(tables[0].shape[::-1], low)]
-        + [cells, modes, modes, modes, modes, cells, cells]
-        + [cells, cells, modes, modes, modes, modes, cells, cells]
+        scratch_shapes=[pltpu.VMEM(each.shape, each.dtype) for each in arrays]
+        + [pltpu.VMEM((size, 2 * MODES * own), low)]
+        + [pltpu.VMEM(each.shape, each.dtype) for each in tables[1:]]
+        + [pltpu.VMEM((2 * MODES * own, size), low)]
+        + [cells, modes, modes, mixed, modes, cells, cells]
+        + [cells, cells, modes, modes, mixed, modes, cells, cells]
         + [
             pltpu.VMEM((size, line_count), wide),
             pltpu.VMEM((STREAMS, 2 * channels, width), low),
@@ -521,7 +564,7 @@
             pltpu.SemaphoreType.DMA((2, STREAMS, n)),
             pltpu.SemaphoreType.DMA((2,)),
             pltpu.SemaphoreType.DMA((2,)),
-            pltpu.SemaphoreType.DMA((9,)),
+            pltpu.SemaphoreType.DMA((8 + tables[0].shape[1],)),
         ],
         compiler_params=pltpu.CompilerParams(
             collective_id=0, has_side_effects=True, vmem_limit_bytes=60 * 1024 * 1024
@@ -553,7 +596,8 @@
         and groups == 2
         and samples == 1
         and slab_rows == ROWS
-        and 2 * (channels // n) == 8
+        and n % HALVES == 0
+        and 2 * (channels // (n // HALVES)) == 16
         and line_count % (128 * STREAMS) == 0
     )
     if fits:

time: 56.8 us -> 50.4 us (0.89)
  Pallas kernels: 52.7 us -> 46.4 us
    pallas_call x1, Pallas kernels: 52.7 us -> 46.4 us  [one_frequency_each(): pl.pallas_call(functools.partial(step_kernel, n), out_shape=(jax.ShapeDty...]
where the time goes in v5:
time: 50.4 us; the launch traced here: 50.1 us
  Pallas kernels  46.4 us (92%)
  local copies, waits for them, and re-layouts  1.68 us (3%)
  other arithmetic  1.41 us (3%)
  between operations  0.69 us (1%)
    pallas_call x1, Pallas kernels, one_frequency_each(): pl.pallas_call(functools.partial(step_kernel, n), out_shape=(jax.ShapeDty...  46.4 us
    unnamed x7, local copies, waits for them, and re-layouts  1.68 us
    sub x1, other arithmetic, adam(): spectral_weight - learn_rate * (first_hat / (jnp.sqrt(second_hat) + epsil...  1.41 us

profile of v5, /device:TPU:0, one launch (start us, length us, event | category | flops | bytes accessed | tf_op | source)
XLA Modules:
  0.0 50.1 jit_solution(469953676214307382)
XLA Ops:
  0.6 0.0 copy-start
  0.6 0.0 copy-start.1
  0.7 0.0 copy-start.2
  0.7 46.4 %shard_map.147 = (bf16[512,256]{1,0:T(8,128)(2,1)}, f32[64,64]{1,0:T(8,128)}) custom-call(bf16[512,256]{1,0:T(8,128)(2,1)} %bitcast.5, bf16[512,256]{1,0:T(8,128)(2,1)} %bitcast.6, f32[64,64]{1,0:T(8,128)} %weight_hbm.1, bf16[64,64]{1,0:T(8,128)(2,1)} %skip_hbm.1, f32[1,64]{1,0:T(1,128)} %bitcast.7, s32[2]{0:T(128)} %counts.1, ...), custom_call_target="tpu_custom_call" | custom-call | flops 1000000000 | bytes 2000000 | tf_op jit(solution)/shard_map/pallas_call | solution.py:541
  47.0 0.0 copy-done
  47.1 0.0 copy-done.1
  47.1 0.0 copy-done.2
  47.1 1.4 %multiply_subtract_fusion = (f32[64,64]{1,0:T(8,128)}, f32[64,64]{1,0:T(8,128)}, f32[64,64]{1,0:T(8,128)}) fusion(f32[64,64]{1,0:T(8,128)S(1)} %copy-done, f32[64,64]{1,0:T(8,128)} %get-tuple-element.7, f32[64,64]{1,0:T(8,128)S(1)} %copy-done.1, f32[64,64]{1,0:T(8,128)S(1)} %copy-done.2), kind=kLoop, calls=%fused_computation.2 | loop fusion | flops 61440 | bytes 114688 | tf_op jit(solution)/shard_map/sub | solution.py:585
  48.5 1.7 %copy.17 = bf16[1,64,8,256]{3,2,1,0:T(8,128)(2,1)} copy(bf16[1,64,8,256]{3,2,1,0:T(8,128)(2,1)} %bitcast.4) | data formatting | bytes 524288
Async XLA Ops:
  0.6 46.4 %copy-start = (f32[64,64]{1,0:T(8,128)S(1)}, f32[64,64]{1,0:T(8,128)}, u32[]{:S(2)}) copy-start(f32[64,64]{1,0:T(8,128)} %weight_hbm.1) | copy-start | bytes 49156
  0.6 46.4 %copy-start.1 = (f32[64,64]{1,0:T(8,128)S(1)}, f32[64,64]{1,0:T(8,128)}, u32[]{:S(2)}) copy-start(f32[64,64]{1,0:T(8,128)} %param.15) | copy-start | bytes 49156
  0.7 46.4 %copy-start.2 = (f32[64,64]{1,0:T(8,128)S(1)}, f32[64,64]{1,0:T(8,128)}, u32[]{:S(2)}) copy-start(f32[64,64]{1,0:T(8,128)} %param.16) | copy-start | bytes 49156

commit v6 on v5

--- a/solution.py
+++ b/solution.py
@@ -198,7 +198,8 @@
     order_hbm,
     order_back_hbm,
     spread_hbm,
-    out,
+    out_rows,
+    out_skip,
     out_grad,
     dens,
     upst,
@@ -224,7 +225,6 @@
     d1s,
     d1r,
     d2s,
-    d2r,
     skip_part,
     kept,
     wsend,
@@ -237,6 +237,7 @@
     pair_send,
     pair_recv,
     load_sem,
+    store_sem,
 ):
     me = lax.axis_index("dom")
     core = lax.axis_index("dp")
@@ -319,7 +320,7 @@
                 half * members + peer,
                 source.at[stream, peer],
                 target.at[stream, member],
-                block_sem.at[stage // 4, stream, shift],
+                block_sem.at[stream, shift],
             ).start()
             return carry
 
@@ -442,7 +443,7 @@
             device = near(step)
             cells = b2r.at[stream, device]
             remote(
-                3, stream, me, cells, cells, block_sem.at[0, stream, members - step]
+                3, stream, me, cells, cells, block_sem.at[stream, members - step]
             ).wait_recv()
             slope_block(device, cells[...])
             remote(
@@ -461,6 +462,8 @@
         send_modes(5, stream, c2s, c2r, n)
     for stream in range(STREAMS):
         skip_part[:, lanes(stream)] = dot(back_map, flat(c1s, stream))
+    skip_store = pltpu.make_async_copy(skip_part, out_skip, store_sem.at[0])
+    skip_store.start()
     products = jnp.zeros((2 * channels, 2 * channels), wide)
     for stream in range(STREAMS):
         all_of(5, stream, c2r).wait_recv()
@@ -484,36 +487,100 @@
         device_id_type=MESH,
     )
     swap_grad.start()
+
+    def own_store(stream):
+        return pltpu.make_async_copy(
+            d2s.at[stream, member],
+            out_rows.at[rows(member), lanes(stream)],
+            store_sem.at[1 + stream],
+        )
+
     for stream in range(STREAMS):
         all_of(6, stream, d1r).wait_recv()
         d2s[stream] = blocks_of(dot(trans_back[...], flat(d1r, stream)), members)
-        send_blocks(7, stream, d2s, d2r)
+
+        def send_last(shift, carry):
+            peer = near(shift)
+            remote(
+                7,
+                stream,
+                half * members + peer,
+                d2s.at[stream, peer],
+                out_rows.at[rows(member), lanes(stream)],
+            ).start()
+            return carry
+
+        lax.fori_loop(1, members, send_last, 0, unroll=True)
+        own_store(stream).start()
     swap_grad.wait_recv()
     out_grad[...] = ours + grecv[...][:, :channels]
     swap.wait_send()
     swap_grad.wait_send()
-    for stage, source in enumerate((a1r, a2r, b1r, b2r, c1r, c2r, d1r)):
+    for stage, source in enumerate((a1r, a2r, b1r, b2r, c1r, c2r, d1r, d2s)):
         for stream in range(STREAMS):
             all_of(stage, stream, source).wait_send()
-    for stream in range(STREAMS):
-
-        def final_block(device, cells):
-            total = cells.astype(wide) + skip_part[rows(device), lanes(stream)]
-            out[rows(device), lanes(stream)] = total.astype(low)
-
-        final_block(member, d2s[stream, member])
-
-        def one_final(step, carry):
-            device = near(step)
-            cells = d2r.at[stream, device]
-            remote(
-                7, stream, me, cells, cells, block_sem.at[1, stream, members - step]
-            ).wait_recv()
-            final_block(device, cells[...])
-            return carry
-
-        lax.fori_loop(1, members, one_final, 0)
-        all_of(7, stream, d2r).wait_send()
+    skip_store.wait()
+    for stream in range(STREAMS):
+        own_store(stream).wait()
+        all_of(7, stream, d2s).wait_recv()
+
+
+def finish_kernel(
+    rows_hbm,
+    skip_hbm,
+    grad_hbm,
+    weight_hbm,
+    first_hbm,
+    second_hbm,
+    out,
+    new_weight,
+    new_first,
+    new_second,
+    rows,
+    skip,
+    grad,
+    weight,
+    first,
+    second,
+    total,
+    one,
+    two,
+    three,
+    load_sem,
+    store_sem,
+):
+    loads = [
+        pltpu.make_async_copy(source, target, load_sem.at[index])
+        for index, (source, target) in enumerate(
+            (
+                (grad_hbm, grad),
+                (weight_hbm, weight),
+                (first_hbm, first),
+                (second_hbm, second),
+                (rows_hbm, rows),
+                (skip_hbm, skip),
+            )
+        )
+    ]
+    for load in loads:
+        load.start()
+    for load in loads[:4]:
+        load.wait()
+    one[...], two[...], three[...] = adam(grad[...], weight[...], first[...], second[...])
+    stores = [
+        pltpu.make_async_copy(source, target, store_sem.at[index])
+        for index, (source, target) in enumerate(
+            ((one, new_weight), (two, new_first), (three, new_second), (total, out))
+        )
+    ]
+    for store in stores[:3]:
+        store.start()
+    for load in loads[4:]:
+        load.wait()
+    total[...] = (rows[...].astype(jnp.float32) + skip[...]).astype(total.dtype)
+    stores[3].start()
+    for store in stores:
+        store.wait()
 
 
 def one_frequency_each(
@@ -538,20 +605,21 @@
         skip_weight,
         skip_bias.reshape(1, channels),
     )
-    input_grad, weight_grad = pl.pallas_call(
+    input_rows, skip_back, weight_grad = pl.pallas_call(
         functools.partial(step_kernel, n),
         out_shape=(
             jax.ShapeDtypeStruct((size, line_count), low),
+            jax.ShapeDtypeStruct((size, line_count), wide),
             jax.ShapeDtypeStruct((channels, channels), wide),
         ),
         in_specs=[hbm] * 5 + [pl.BlockSpec(memory_space=pltpu.SMEM)] + [hbm] * 4,
-        out_specs=(vmem,) * 2,
+        out_specs=(hbm, hbm, vmem),
         scratch_shapes=[pltpu.VMEM(each.shape, each.dtype) for each in arrays]
         + [pltpu.VMEM((size, 2 * MODES * own), low)]
         + [pltpu.VMEM(each.shape, each.dtype) for each in tables[1:]]
         + [pltpu.VMEM((2 * MODES * own, size), low)]
         + [cells, modes, modes, mixed, modes, cells, cells]
-        + [cells, cells, modes, modes, mixed, modes, cells, cells]
+        + [cells, cells, modes, modes, mixed, modes, cells]
         + [
             pltpu.VMEM((size, line_count), wide),
             pltpu.VMEM((STREAMS, 2 * channels, width), low),
@@ -561,10 +629,11 @@
             pltpu.VMEM((channels, 2 * channels), wide),
             pltpu.SemaphoreType.DMA((8, STREAMS)),
             pltpu.SemaphoreType.DMA((8, STREAMS)),
-            pltpu.SemaphoreType.DMA((2, STREAMS, n)),
+            pltpu.SemaphoreType.DMA((STREAMS, members)),
             pltpu.SemaphoreType.DMA((2,)),
             pltpu.SemaphoreType.DMA((2,)),
             pltpu.SemaphoreType.DMA((8 + tables[0].shape[1],)),
+            pltpu.SemaphoreType.DMA((1 + STREAMS,)),
         ],
         compiler_params=pltpu.CompilerParams(
             collective_id=0, has_side_effects=True, vmem_limit_bytes=60 * 1024 * 1024
@@ -573,7 +642,24 @@
             flops=1_000_000_000, bytes_accessed=2_000_000, transcendentals=300_000
         ),
     )(*arrays, mode_counts, *tables)
-    updated = adam(weight_grad, spectral_weight, moment_one, moment_two)
+    square = jax.ShapeDtypeStruct((channels, channels), wide)
+    input_grad, *updated = pl.pallas_call(
+        finish_kernel,
+        out_shape=(jax.ShapeDtypeStruct((size, line_count), low), square, square, square),
+        in_specs=[hbm] * 6,
+        out_specs=(hbm,) * 4,
+        scratch_shapes=[
+            pltpu.VMEM((size, line_count), low),
+            pltpu.VMEM((size, line_count), wide),
+            *[pltpu.VMEM((channels, channels), wide)] * 4,
+            pltpu.VMEM((size, line_count), low),
+            *[pltpu.VMEM((channels, channels), wide)] * 3,
+            pltpu.SemaphoreType.DMA((6,)),
+            pltpu.SemaphoreType.DMA((4,)),
+        ],
+        compiler_params=pltpu.CompilerParams(vmem_limit_bytes=60 * 1024 * 1024),
+        cost_estimate=pl.CostEstimate(flops=300_000, bytes_accessed=1_200_000, transcendentals=0),
+    )(input_rows, skip_back, weight_grad, spectral_weight, moment_one, moment_two)
     return (input_grad.reshape(density.shape), *updated)
 
 

time: 50.4 us -> 48.7 us (0.966)
  local copies, waits for them, and re-layouts: 1.68 us -> 0 us
  Pallas kernels: 46.4 us -> 47.9 us
  other arithmetic: 1.41 us -> 0 us
    pallas_call x0 -> x1, Pallas kernels: none -> 2.04 us  [one_frequency_each(): pl.pallas_call(finish_kernel, out_shape=(jax.ShapeDtypeStruct((size, line...]
    unnamed x7 -> x0, local copies, waits for them, and re-layouts: 1.68 us -> none
    sub x1 -> x0, other arithmetic: 1.41 us -> none  [adam(): spectral_weight - learn_rate * (first_hat / (jnp.sqrt(second_hat) + epsil...]
where the time goes in v6:
time: 48.7 us; the launch traced here: 48.6 us
  Pallas kernels  47.9 us (98%)
  between operations  0.64 us (1%)
    pallas_call x1, Pallas kernels, one_frequency_each(): pl.pallas_call(functools.partial(step_kernel, n), out_shape=(jax.ShapeDty...  45.9 us
    pallas_call x1, Pallas kernels, one_frequency_each(): pl.pallas_call(finish_kernel, out_shape=(jax.ShapeDtypeStruct((size, line...  2.04 us

profile of v6, /device:TPU:0, one launch (start us, length us, event | category | flops | bytes accessed | tf_op | source)
XLA Modules:
  0.0 48.6 jit_solution(6263504921038282607)
XLA Ops:
  0.6 45.9 %shard_map.147 = (bf16[512,256]{1,0:T(8,128)(2,1)}, f32[512,256]{1,0:T(8,128)}, f32[64,64]{1,0:T(8,128)}) custom-call(bf16[512,256]{1,0:T(8,128)(2,1)} %bitcast.4, bf16[512,256]{1,0:T(8,128)(2,1)} %bitcast.5, f32[64,64]{1,0:T(8,128)} %weight_hbm.3, bf16[64,64]{1,0:T(8,128)(2,1)} %skip_hbm.1, f32[1,64]{1,0:T(1,128)} %bitcast.7, s32[2]{0:T(128)} %counts.1, ...), custom_call_target="tpu_custom_call" | custom-call | flops 1000000000 | bytes 2000000 | tf_op jit(solution)/shard_map/pallas_call | solution.py:608
  46.5 2.0 %shard_map.148 = (bf16[512,256]{1,0:T(8,128)(2,1)}, f32[64,64]{1,0:T(8,128)}, f32[64,64]{1,0:T(8,128)}, f32[64,64]{1,0:T(8,128)}) custom-call(bf16[512,256]{1,0:T(8,128)(2,1)} %get-tuple-element.11.rows_hbm, f32[512,256]{1,0:T(8,128)} %get-tuple-element.12.skip_hbm, f32[64,64]{1,0:T(8,128)} %get-tuple-element.13.grad_hbm, f32[64,64]{1,0:T(8,128)} %weight_hbm.3, ...), custom_call_target="tpu_custom_call" | custom-call | flops 300000 | bytes 1200000 | tf_op jit(solution)/shard_map/pallas_call | solution.py:646

commit v7 on v6

--- a/solution.py
+++ b/solution.py
@@ -163,7 +163,8 @@
     parts = parts.reshape(halves, members, 1, rows, MODES, 2, 1)
     same = np.eye(own).reshape(1, 1, own, 1, 1, 1, own)
     transform = (parts * same).reshape(halves, members * own * rows, -1, LANES)
-    transform = transform.transpose(0, 2, 1, 3)
+    turned = transform.transpose(0, 2, 3, 1).reshape(halves, MODES * 2 * own, -1, LANES)
+    transform, turned = transform.transpose(0, 2, 1, 3), turned.transpose(0, 2, 1, 3)
     channels = members * own
     order = np.zeros((2, members, own, members, 2, own))
     for part in range(2):
@@ -173,7 +174,7 @@
     order = order.reshape(2 * channels, 2 * channels)
     spread = np.repeat(np.eye(channels), rows, axis=0)
     low = lambda table: jnp.asarray(table.astype(np.float32), jnp.bfloat16)
-    return low(transform), low(order), low(order.T), low(spread)
+    return low(transform), low(turned), low(order), low(order.T), low(spread)
 
 
 def dot(left, right, dims=((1,), (0,))):
@@ -195,6 +196,7 @@
     bias_hbm,
     counts,
     trans_back_hbm,
+    trans_hbm,
     order_hbm,
     order_back_hbm,
     spread_hbm,
@@ -207,10 +209,10 @@
     skip,
     bias,
     trans_back,
+    trans,
     order,
     order_back,
     spread,
-    trans,
     a1r,
     a2s,
     a2r,
@@ -260,6 +262,10 @@
                 (order_hbm, order),
                 (order_back_hbm, order_back),
                 *(
+                    (trans_hbm.at[half, tile], trans.at[:, pl.ds(tile * LANES, LANES)])
+                    for tile in range(trans_hbm.shape[1])
+                ),
+                *(
                     (trans_back_hbm.at[half, tile], trans_back.at[:, pl.ds(tile * LANES, LANES)])
                     for tile in range(trans_back_hbm.shape[1])
                 ),
@@ -377,7 +383,6 @@
         full = dot(tall, spread[...], ((1,), (1,)))
         return jnp.where(same_row, full, 0.0).astype(low)
 
-    trans[...] = trans_back[...].astype(wide).T.astype(low)
     forward_map = wide_map(((1,), (0,)))
     swap.wait_recv()
     mine = weight[...].astype(low).astype(wide)
@@ -439,12 +444,10 @@
         slope_block(member, b2s[stream, member])
         c1r[stream, member] = c1s[stream, member]
 
-        def one_slope(step, carry):
-            device = near(step)
+        def one_slope(shift, carry):
+            device = near(members - shift)
             cells = b2r.at[stream, device]
-            remote(
-                3, stream, me, cells, cells, block_sem.at[stream, members - step]
-            ).wait_recv()
+            remote(3, stream, me, cells, cells, block_sem.at[stream, shift]).wait_recv()
             slope_block(device, cells[...])
             remote(
                 4,
@@ -455,7 +458,7 @@
             ).start()
             return carry
 
-        lax.fori_loop(1, members, one_slope, 0)
+        lax.fori_loop(1, members, one_slope, 0, unroll=True)
     for stream in range(STREAMS):
         all_of(4, stream, c1r).wait_recv()
         c2s[stream] = blocks_of(dot(trans[...], flat(c1r, stream)), n)
@@ -612,12 +615,12 @@
             jax.ShapeDtypeStruct((size, line_count), wide),
             jax.ShapeDtypeStruct((channels, channels), wide),
         ),
-        in_specs=[hbm] * 5 + [pl.BlockSpec(memory_space=pltpu.SMEM)] + [hbm] * 4,
+        in_specs=[hbm] * 5 + [pl.BlockSpec(memory_space=pltpu.SMEM)] + [hbm] * 5,
         out_specs=(hbm, hbm, vmem),
         scratch_shapes=[pltpu.VMEM(each.shape, each.dtype) for each in arrays]
         + [pltpu.VMEM((size, 2 * MODES * own), low)]
-        + [pltpu.VMEM(each.shape, each.dtype) for each in tables[1:]]
         + [pltpu.VMEM((2 * MODES * own, size), low)]
+        + [pltpu.VMEM(each.shape, each.dtype) for each in tables[2:]]
         + [cells, modes, modes, mixed, modes, cells, cells]
         + [cells, cells, modes, modes, mixed, modes, cells]
         + [
@@ -632,7 +635,7 @@
             pltpu.SemaphoreType.DMA((STREAMS, members)),
             pltpu.SemaphoreType.DMA((2,)),
             pltpu.SemaphoreType.DMA((2,)),
-            pltpu.SemaphoreType.DMA((8 + tables[0].shape[1],)),
+            pltpu.SemaphoreType.DMA((8 + tables[0].shape[1] + tables[1].shape[1],)),
             pltpu.SemaphoreType.DMA((1 + STREAMS,)),
         ],
         compiler_params=pltpu.CompilerParams(

time: 48.7 us -> 49.8 us (1.023)
  Pallas kernels: 47.9 us -> 49 us
    pallas_call x1, Pallas kernels: 45.9 us -> 46.9 us  [one_frequency_each(): pl.pallas_call(functools.partial(step_kernel, n), out_shape=(jax.ShapeDty...]
where the time goes in v7:
time: 49.8 us; the launch traced here: 49.6 us
  Pallas kernels  49 us (98%)
  between operations  0.64 us (1%)
    pallas_call x1, Pallas kernels, one_frequency_each(): pl.pallas_call(functools.partial(step_kernel, n), out_shape=(jax.ShapeDty...  46.9 us
    pallas_call x1, Pallas kernels, one_frequency_each(): pl.pallas_call(finish_kernel, out_shape=(jax.ShapeDtypeStruct((size, line...  2.04 us

profile of v7, /device:TPU:0, one launch (start us, length us, event | category | flops | bytes accessed | tf_op | source)
XLA Modules:
  0.0 49.6 jit_solution(14032930215660795903)
XLA Ops:
  0.6 46.9 %shard_map.156 = (bf16[512,256]{1,0:T(8,128)(2,1)}, f32[512,256]{1,0:T(8,128)}, f32[64,64]{1,0:T(8,128)}) custom-call(bf16[512,256]{1,0:T(8,128)(2,1)} %bitcast.4, bf16[512,256]{1,0:T(8,128)(2,1)} %bitcast.5, f32[64,64]{1,0:T(8,128)} %weight_hbm.3, bf16[64,64]{1,0:T(8,128)(2,1)} %skip_hbm.1, f32[1,64]{1,0:T(1,128)} %bitcast.7, s32[2]{0:T(128)} %counts.1, ...), custom_call_target="tpu_custom_call" | custom-call | flops 1000000000 | bytes 2000000 | tf_op jit(solution)/shard_map/pallas_call | solution.py:611
  47.6 2.0 %shard_map.157 = (bf16[512,256]{1,0:T(8,128)(2,1)}, f32[64,64]{1,0:T(8,128)}, f32[64,64]{1,0:T(8,128)}, f32[64,64]{1,0:T(8,128)}) custom-call(bf16[512,256]{1,0:T(8,128)(2,1)} %get-tuple-element.11.rows_hbm, f32[512,256]{1,0:T(8,128)} %get-tuple-element.12.skip_hbm, f32[64,64]{1,0:T(8,128)} %get-tuple-element.13.grad_hbm, f32[64,64]{1,0:T(8,128)} %weight_hbm.3, ...), custom_call_target="tpu_custom_call" | custom-call | flops 300000 | bytes 1200000 | tf_op jit(solution)/shard_map/pallas_call | solution.py:649

commit v8 on v6

--- a/solution.py
+++ b/solution.py
@@ -151,6 +151,7 @@
 STREAMS = 2
 HALVES = 2
 LANES = 128
+CHUNKS = 4
 
 
 def fixed_tables(halves, members, own, rows):
@@ -439,12 +440,10 @@
         slope_block(member, b2s[stream, member])
         c1r[stream, member] = c1s[stream, member]
 
-        def one_slope(step, carry):
-            device = near(step)
+        def one_slope(shift, carry):
+            device = near(members - shift)
             cells = b2r.at[stream, device]
-            remote(
-                3, stream, me, cells, cells, block_sem.at[stream, members - step]
-            ).wait_recv()
+            remote(3, stream, me, cells, cells, block_sem.at[stream, shift]).wait_recv()
             slope_block(device, cells[...])
             remote(
                 4,
@@ -557,29 +556,41 @@
                 (weight_hbm, weight),
                 (first_hbm, first),
                 (second_hbm, second),
-                (rows_hbm, rows),
-                (skip_hbm, skip),
             )
         )
     ]
+    step = rows.shape[0] // CHUNKS
+    parts = [pl.ds(chunk * step, step) for chunk in range(CHUNKS)]
+    row_loads = [
+        [
+            pltpu.make_async_copy(source.at[part], target.at[part], load_sem.at[4 + 2 * chunk + k])
+            for k, (source, target) in enumerate(((rows_hbm, rows), (skip_hbm, skip)))
+        ]
+        for chunk, part in enumerate(parts)
+    ]
+    row_stores = [
+        pltpu.make_async_copy(total.at[part], out.at[part], store_sem.at[3 + chunk])
+        for chunk, part in enumerate(parts)
+    ]
+    for load in loads + [each for pair in row_loads for each in pair]:
+        load.start()
+    for part, pair, store in zip(parts, row_loads, row_stores):
+        for load in pair:
+            load.wait()
+        total[part] = (rows[part].astype(jnp.float32) + skip[part]).astype(total.dtype)
+        store.start()
     for load in loads:
-        load.start()
-    for load in loads[:4]:
         load.wait()
     one[...], two[...], three[...] = adam(grad[...], weight[...], first[...], second[...])
     stores = [
         pltpu.make_async_copy(source, target, store_sem.at[index])
         for index, (source, target) in enumerate(
-            ((one, new_weight), (two, new_first), (three, new_second), (total, out))
+            ((one, new_weight), (two, new_first), (three, new_second))
         )
     ]
-    for store in stores[:3]:
+    for store in stores:
         store.start()
-    for load in loads[4:]:
-        load.wait()
-    total[...] = (rows[...].astype(jnp.float32) + skip[...]).astype(total.dtype)
-    stores[3].start()
-    for store in stores:
+    for store in row_stores + stores:
         store.wait()
 
 
@@ -654,8 +665,8 @@
             *[pltpu.VMEM((channels, channels), wide)] * 4,
             pltpu.VMEM((size, line_count), low),
             *[pltpu.VMEM((channels, channels), wide)] * 3,
-            pltpu.SemaphoreType.DMA((6,)),
-            pltpu.SemaphoreType.DMA((4,)),
+            pltpu.SemaphoreType.DMA((4 + 2 * CHUNKS,)),
+            pltpu.SemaphoreType.DMA((3 + CHUNKS,)),
         ],
         compiler_params=pltpu.CompilerParams(vmem_limit_bytes=60 * 1024 * 1024),
         cost_estimate=pl.CostEstimate(flops=300_000, bytes_accessed=1_200_000, transcendentals=0),

time: 48.7 us -> 49.2 us (1.010)
  Pallas kernels: 47.9 us -> 48.4 us
where the time goes in v8:
time: 49.2 us; the launch traced here: 49 us
  Pallas kernels  48.4 us (98%)
  between operations  0.64 us (1%)
    pallas_call x1, Pallas kernels, one_frequency_each(): pl.pallas_call(functools.partial(step_kernel, n), out_shape=(jax.ShapeDty...  46.3 us
    pallas_call x1, Pallas kernels, one_frequency_each(): pl.pallas_call(finish_kernel, out_shape=(jax.ShapeDtypeStruct((size, line...  2.11 us

profile of v8, /device:TPU:0, one launch (start us, length us, event | category | flops | bytes accessed | tf_op | source)
XLA Modules:
  0.0 49.0 jit_solution(8350455846796846652)
XLA Ops:
  0.6 46.3 %shard_map.147 = (bf16[512,256]{1,0:T(8,128)(2,1)}, f32[512,256]{1,0:T(8,128)}, f32[64,64]{1,0:T(8,128)}) custom-call(bf16[512,256]{1,0:T(8,128)(2,1)} %bitcast.4, bf16[512,256]{1,0:T(8,128)(2,1)} %bitcast.5, f32[64,64]{1,0:T(8,128)} %weight_hbm.3, bf16[64,64]{1,0:T(8,128)(2,1)} %skip_hbm.1, f32[1,64]{1,0:T(1,128)} %bitcast.7, s32[2]{0:T(128)} %counts.1, ...), custom_call_target="tpu_custom_call" | custom-call | flops 1000000000 | bytes 2000000 | tf_op jit(solution)/shard_map/pallas_call | solution.py:619
  46.9 2.1 %shard_map.148 = (bf16[512,256]{1,0:T(8,128)(2,1)}, f32[64,64]{1,0:T(8,128)}, f32[64,64]{1,0:T(8,128)}, f32[64,64]{1,0:T(8,128)}) custom-call(bf16[512,256]{1,0:T(8,128)(2,1)} %get-tuple-element.11.rows_hbm, f32[512,256]{1,0:T(8,128)} %get-tuple-element.12.skip_hbm, f32[64,64]{1,0:T(8,128)} %get-tuple-element.13.grad_hbm, f32[64,64]{1,0:T(8,128)} %weight_hbm.3, ...), custom_call_target="tpu_custom_call" | custom-call | flops 300000 | bytes 1200000 | tf_op jit(solution)/shard_map/pallas_call | solution.py:657

commit v9 on v6

--- a/solution.py
+++ b/solution.py
@@ -278,7 +278,7 @@
         )
         return carry
 
-    lax.fori_loop(1, n, greet, 0, unroll=True)
+    lax.fori_loop(1, n, greet, 0)
     pl.semaphore_signal(barrier, inc=1, device_id=(1 - core, me), device_id_type=MESH)
     pl.semaphore_wait(barrier, n)
     loads[0].wait()
@@ -305,7 +305,7 @@
             ).start()
             return carry
 
-        lax.fori_loop(1, n, one, 0, unroll=True)
+        lax.fori_loop(1, n, one, 0)
         target[stream, me] = source[stream, lax.rem(me, slots)]
 
     def near(step):
@@ -324,7 +324,7 @@
             ).start()
             return carry
 
-        lax.fori_loop(1, members, one, 0, unroll=True)
+        lax.fori_loop(1, members, one, 0)
 
     def all_of(stage, stream, ref):
         blocks = ref.at[stream, pl.ds(0, ref.shape[1] - 1)]
@@ -349,7 +349,7 @@
             ).start()
             return carry
 
-        lax.fori_loop(1, members, start_one, 0, unroll=True)
+        lax.fori_loop(1, members, start_one, 0)
         a1r[stream, member] = dens[rows(member), lanes(stream)]
 
     loads[1].wait()
@@ -510,7 +510,7 @@
             ).start()
             return carry
 
-        lax.fori_loop(1, members, send_last, 0, unroll=True)
+        lax.fori_loop(1, members, send_last, 0)
         own_store(stream).start()
     swap_grad.wait_recv()
     out_grad[...] = ours + grecv[...][:, :channels]

time: 48.7 us -> 48.6 us (level)
  no operation moved by 1% of the time
where the time goes in v9:
time: 48.6 us; the launch traced here: 48.5 us
  Pallas kernels  47.8 us (98%)
  between operations  0.64 us (1%)
    pallas_call x1, Pallas kernels, one_frequency_each(): pl.pallas_call(functools.partial(step_kernel, n), out_shape=(jax.ShapeDty...  45.8 us
    pallas_call x1, Pallas kernels, one_frequency_each(): pl.pallas_call(finish_kernel, out_shape=(jax.ShapeDtypeStruct((size, line...  2.04 us

profile of v9, /device:TPU:0, one launch (start us, length us, event | category | flops | bytes accessed | tf_op | source)
XLA Modules:
  0.0 48.5 jit_solution(8134705667666179316)
XLA Ops:
  0.6 45.8 %shard_map.147 = (bf16[512,256]{1,0:T(8,128)(2,1)}, f32[512,256]{1,0:T(8,128)}, f32[64,64]{1,0:T(8,128)}) custom-call(bf16[512,256]{1,0:T(8,128)(2,1)} %bitcast.4, bf16[512,256]{1,0:T(8,128)(2,1)} %bitcast.5, f32[64,64]{1,0:T(8,128)} %weight_hbm.3, bf16[64,64]{1,0:T(8,128)(2,1)} %skip_hbm.1, f32[1,64]{1,0:T(1,128)} %bitcast.7, s32[2]{0:T(128)} %counts.1, ...), custom_call_target="tpu_custom_call" | custom-call | flops 1000000000 | bytes 2000000 | tf_op jit(solution)/shard_map/pallas_call | solution.py:608
  46.5 2.0 %shard_map.148 = (bf16[512,256]{1,0:T(8,128)(2,1)}, f32[64,64]{1,0:T(8,128)}, f32[64,64]{1,0:T(8,128)}, f32[64,64]{1,0:T(8,128)}) custom-call(bf16[512,256]{1,0:T(8,128)(2,1)} %get-tuple-element.11.rows_hbm, f32[512,256]{1,0:T(8,128)} %get-tuple-element.12.skip_hbm, f32[64,64]{1,0:T(8,128)} %get-tuple-element.13.grad_hbm, f32[64,64]{1,0:T(8,128)} %weight_hbm.3, ...), custom_call_target="tpu_custom_call" | custom-call | flops 300000 | bytes 1200000 | tf_op jit(solution)/shard_map/pallas_call | solution.py:646
